TPU v7x, 128 devices: a whole 4x4x4 slice. The times are simulated.
128 devices in a mesh: tm: 64 (over z, y, x), space: 2 (over core).
Axes of the slice: x: 4, y: 4, z: 4, core: 2. Of those that a mesh axis runs over, the one named last changes fastest.
Arguments:
- snapshots: bfloat16 [32768, 16384], P('tm', 'space'), may hold values from -40 to 40
- exponents: float32 [2, 32], replicated, may hold values from -150 to 150, as said below
Outputs:
- new_exponents: float32 [2, 32], replicated
- amplitudes: float32 [2, 32, 16384], P(None, None, 'space')
- residual: bfloat16 [32768, 16384], P('tm', 'space')
Inputs may be any that keep to these rules, and one draw needn't show every extreme that they name: `exponents`: row 0 lies in -2.3 to 0.8, row 1 in -150 to 150.
All inputs are finite; a program needn't handle non-finite values.
Results may differ from a plain program's by a relative error of at most 0.0012.
The roundings to bfloat16 on the way count: a program that leaves them out, or rounds other values in their place, can miss the bound.
Values sent between devices are 32-bit elements; how exact they have to be, the bound alone decides.
No kernel may reach another device: no remote copies, remote signals or barrier semaphores. Data moves between devices by JAX's collectives and lax.ppermute only.
A program may use at most 64 MiB of HBM per device.

v0:
```python
import jax
import jax.numpy as jnp
from jax import lax
from jax.sharding import PartitionSpec as P

damping = 0.01


def factor_solve(factor, right):
    lower_part = lax.linalg.triangular_solve(factor, right, left_side=True, lower=True)
    return lax.linalg.triangular_solve(
        factor, lower_part, left_side=True, lower=True, transpose_a=True
    )


def make_basis(exponents, time_grid):
    magnitude = jnp.exp(time_grid[:, None] * exponents[0][None, :])
    phase_angle = time_grid[:, None] * exponents[1][None, :]
    plain = jnp.concatenate([magnitude * jnp.cos(phase_angle), magnitude * jnp.sin(phase_angle)], 1)
    return jnp.concatenate([plain, time_grid[:, None] * plain], 1)


def inner_product(left, right):
    return lax.dot_general(
        left,
        right,
        (((0,), (0,)), ((), ())),
        precision=lax.Precision.HIGHEST,
        preferred_element_type=jnp.float32,
    )


def hermitian(blocks, modes):
    return (
        blocks[:modes, :modes] + blocks[modes:, modes:],
        blocks[:modes, modes:] - blocks[modes:, :modes],
    )


def embedded(real_part, imag_part):
    return jnp.concatenate(
        [jnp.concatenate([real_part, -imag_part], 1), jnp.concatenate([imag_part, real_part], 1)], 0
    )


def sign_flip(modes):
    return jnp.concatenate([jnp.ones((modes,), jnp.float32), -jnp.ones((modes,), jnp.float32)])


def basis_solve(gram_matrix, modes):
    double = 2 * modes
    g_real, g_imag = hermitian(gram_matrix[:double, :double], modes)
    factor = jnp.linalg.cholesky(embedded(g_real, g_imag))
    return factor_solve(factor, jnp.eye(double, dtype=jnp.float32))


def amplitude_rows(inverse_g, projections, modes):
    left_solve = inverse_g * sign_flip(modes)[None, :]
    return lax.dot_general(
        left_solve,
        projections[:, : 2 * modes],
        (((1,), (1,)), ((), ())),
        precision=lax.Precision.HIGHEST,
        preferred_element_type=jnp.float32,
    )


def self_only(amp_rows):
    return lax.dot_general(
        amp_rows,
        amp_rows,
        (((1,), (1,)), ((), ())),
        precision=lax.Precision.HIGHEST,
        preferred_element_type=jnp.float32,
    )


def fit_terms(amp_rows, projections, modes):
    double = 2 * modes
    self_terms = self_only(amp_rows)
    cross = (
        jnp.dot(
            amp_rows,
            projections[:, double:],
            precision=lax.Precision.HIGHEST,
            preferred_element_type=jnp.float32,
        )
        * sign_flip(modes)[None, :]
    )
    v_real = jnp.diagonal(cross[:modes, :modes]) + jnp.diagonal(cross[modes:, modes:])
    v_imag = jnp.diagonal(cross[:modes, modes:]) - jnp.diagonal(cross[modes:, :modes])
    return (self_terms, jnp.stack([v_real, v_imag]))


def lm_update(exponents, gram_matrix, inverse_g, self_terms, cross_sums, modes):
    double = 2 * modes
    c_real, c_imag = hermitian(gram_matrix[:double, double:], modes)
    e_real, e_imag = hermitian(gram_matrix[double:, double:], modes)
    coupling = embedded(c_real, c_imag)
    through = jnp.dot(coupling.T, inverse_g, precision=lax.Precision.HIGHEST)
    reduced = embedded(e_real, e_imag) - jnp.dot(through, coupling, precision=lax.Precision.HIGHEST)
    m_real = reduced[:modes, :modes]
    m_imag = reduced[modes:, :modes]
    s_real, s_imag = hermitian(self_terms, modes)
    w_real = jnp.sum(c_real.T * s_real + c_imag.T * s_imag, 1)
    w_imag = jnp.sum(c_real.T * s_imag - c_imag.T * s_real, 1)
    grad_real = w_real - cross_sums[0]
    grad_imag = w_imag - cross_sums[1]
    h_real = s_real * m_real - s_imag * m_imag + damping * jnp.eye(modes, dtype=jnp.float32)
    h_imag = s_real * m_imag + s_imag * m_real
    factor = jnp.linalg.cholesky(embedded(h_real, h_imag))
    step_vector = factor_solve(factor, jnp.concatenate([grad_real, grad_imag])[:, None])[:, 0]
    return exponents - jnp.stack([step_vector[:modes], step_vector[modes:]])


def shards(snapshots, exponents):
    local_rows = snapshots.shape[0]
    columns = snapshots.shape[1]
    modes = exponents.shape[1]
    groups = lax.axis_size("tm")
    all_rows = local_rows * groups
    first_row = lax.axis_index("tm") * local_rows
    grid_local = (first_row + jnp.arange(local_rows, dtype=jnp.int32)).astype(
        jnp.float32
    ) / all_rows
    basis = make_basis(exponents, grid_local)
    gram_matrix = lax.psum(inner_product(basis, basis), "tm")
    basis_b = basis.astype(jnp.bfloat16)
    inverse_g = basis_solve(gram_matrix, modes)
    local_proj = lax.dot_general(
        snapshots, basis_b, (((0,), (0,)), ((), ())), preferred_element_type=jnp.float32
    )
    projections = lax.psum(local_proj, "tm")
    amp_rows = amplitude_rows(inverse_g, projections, modes)
    self_terms, cross_sums = fit_terms(amp_rows, projections, modes)
    self_terms, cross_sums = lax.psum((self_terms, cross_sums), "space")
    new_exponents = lm_update(exponents, gram_matrix, inverse_g, self_terms, cross_sums, modes)
    signed = (amp_rows * sign_flip(modes)[:, None]).astype(jnp.bfloat16)
    fitted = jnp.dot(basis_b[:, : 2 * modes], signed, preferred_element_type=jnp.float32)
    residual = (snapshots.astype(jnp.float32) - fitted).astype(jnp.bfloat16)
    return (new_exponents, amp_rows.reshape(2, modes, columns), residual)


def solution(mesh):
    return jax.shard_map(
        shards,
        mesh=mesh,
        in_specs=(P("tm", "space"), P()),
        out_specs=(P(), P(None, None, "space"), P("tm", "space")),
        check_vma=False,
    )
```

profile of v0, /device:TPU:1, one launch (start us, length us, event | category | flops | bytes accessed | tf_op | source)
XLA Modules:
  0.0 217.4 jit_solution(116096414169436430)
XLA Ops:
  7.2 0.8 slice_bitcast_fusion.3
  8.0 0.3 fusion.10
  8.3 1.0 fusion.9
  9.4 6.8 %convolution_bitcast_fusion = f32[8192,128]{0,1:T(8,128)} fusion(bf16[512,128]{0,1:T(8,128)(2,1)S(1)} %fusion.8, bf16[512,8192]{1,0:T(8,128)(2,1)} %param.3), kind=kOutput, calls=%fused_computation.5 | convolution fusion | flops 1073741824 | bytes 12713984 | tf_op jit(solution)/shard_map/dot_general | solution.py:130
  16.2 141.8 %all-reduce.4.cloned.1.call-done = (f32[8192,128]{0,1:T(8,128)}, f32[128,128]{1,0:T(8,128)}) async-done(((f32[8192,128]{0,1:T(8,128)}, f32[128,128]{1,0:T(8,128)}), (f32[8192,128]{0,1:T(8,128)}, f32[128,128]{1,0:T(8,128)})) %all-reduce.4.cloned.1.call-update) | async-done | bytes 4259856 | tf_op jit(solution)/shard_map/psum | solution.py:133
  157.9 0.9 fusion.39
  159.2 5.9 %cholesky.44 = f32[64,64]{1,0:T(8,128)S(1)} custom-call(f32[64,64]{1,0:T(8,128)S(1)} %copy.18), custom_call_target="Cholesky" | custom-call | tf_op jit(solution)/shard_map/jit(cholesky)/cholesky | solution.py:53
  165.1 0.6 compare_reduce_fusion.1
  165.7 0.7 fusion.13
  166.4 4.9 %custom-call.12 = f32[1,64,64]{1,2,0:T(8,128)S(1)} custom-call(f32[1,64,64]{2,1,0:T(8,128)S(1)} %fusion.13), custom_call_target="InvertDiagBlocksLowerTriangular" | custom-call | tf_op jit(solution)/shard_map/triangular_solve | solution.py:11
  171.3 0.2 fusion.20
  171.5 0.2 fusion.18
  171.7 3.6 %fusion.2 = f32[64,8192]{1,0:T(8,128)S(1)} fusion(f32[8192,128]{0,1:T(8,128)} %get-tuple-element.6, f32[64,64]{1,0:T(8,128)S(1)} %fusion.18, f32[64]{0:T(128)S(1)} %copy-done.3), kind=kOutput, calls=%fused_computation.8 | convolution fusion | flops 402657280 | bytes 4210944 | tf_op jit(solution)/shard_map/dot_general | solution.py:59
  175.4 1.8 fusion.4
  177.2 1.8 fusion.43
  179.0 9.2 %subtract_convert_fusion = bf16[512,8192]{1,0:T(8,128)(2,1)} fusion(bf16[512,8192]{1,0:T(8,128)(2,1)} %param.3, f32[64,8192]{1,0:T(8,128)S(1)} %fusion.2, f32[64]{0:T(128)S(1)} %copy-done.3, bf16[512,128]{0,1:T(8,128)(2,1)S(1)} %fusion.8), kind=kOutput, calls=%fused_computation.4 | convolution fusion | flops 550502400 | bytes 18940416 | tf_op jit(solution)/shard_map/dot_general | solution.py:139
  188.3 0.7 gather_fusion.1
  189.0 0.7 gather_fusion.3
  189.7 0.9 gather_fusion.2
  190.6 0.7 gather_fusion
  191.4 4.9 %all-reduce.1 = (f32[64,64]{0,1:T(8,128)S(1)}, f32[2,32]{1,0:T(2,128)S(1)}) all-reduce(f32[64,64]{0,1:T(8,128)S(1)} %fusion.43, f32[2,32]{1,0:T(2,128)S(1)} %pad_maximum_fusion.2), channel_id=1, replica_groups=mesh['tm'=64,'space'=2] {'space'}, use_global_device_ids=true, to_apply=%region_4.6 | all-reduce | flops 4160 | bytes 33280 | tf_op jit(solution)/shard_map/psum | solution.py:136
  196.3 0.1 fusion.27
  196.4 0.3 fusion.31
  196.7 0.2 convolution_subtract_fusion
  197.3 0.1 fusion.17
  197.4 5.9 %cholesky.55 = f32[64,64]{1,0:T(8,128)S(1)} custom-call(f32[64,64]{1,0:T(8,128)S(1)} %fusion.17), custom_call_target="Cholesky" | custom-call | tf_op jit(solution)/shard_map/jit(cholesky)/cholesky | solution.py:111
  203.3 0.6 compare_reduce_fusion
  203.9 0.7 fusion.14
  204.6 4.9 %custom-call.13 = f32[1,64,64]{1,2,0:T(8,128)S(1)} custom-call(f32[1,64,64]{2,1,0:T(8,128)S(1)} %fusion.14), custom_call_target="InvertDiagBlocksLowerTriangular" | custom-call | tf_op jit(solution)/shard_map/triangular_solve | solution.py:11
  209.5 0.2 convolution_bitcast_fusion.2
  209.7 0.2 convolution_bitcast_fusion.1
  209.9 0.6 maximum_subtract_fusion
  (34 shorter events, 1.0 us)
Async XLA Ops:
  7.2 150.8 %all-reduce.4.cloned.1.call-start = ((), (), s32[]{:S(2)}) async-start(), calls=%async_computation | async-start | bytes 8519680 | tf_op jit(solution)/shard_map/psum | solution.py:133
  16.1 155.6 %copy-start.3 = (f32[64]{0:T(128)S(1)}, f32[64]{0:T(128)}, u32[]{:S(2)}) copy-start(f32[64]{0:T(128)} %constant.72.clone.1) | copy-start | bytes 772
  171.7 3.7 %copy-start.1 = (f32[8192,128]{0,1:T(8,128)S(1)}, f32[8192,128]{0,1:T(8,128)}, u32[]{:S(2)}) copy-start(f32[8192,128]{0,1:T(8,128)} %get-tuple-element.6) | copy-start | bytes 12582916
  175.4 3.6 %copy-start = (f32[64,8192]{1,0:T(8,128)}, f32[64,8192]{1,0:T(8,128)S(1)}, u32[]{:S(2)}) copy-start(f32[64,8192]{1,0:T(8,128)S(1)} %fusion.2) | copy-start | bytes 6291460
  188.2 8.0 %copy-start.2 = (f32[128,128]{1,0:T(8,128)S(1)}, f32[128,128]{1,0:T(8,128)}, u32[]{:S(2)}) copy-start(f32[128,128]{1,0:T(8,128)} %get-tuple-element.7) | copy-start | bytes 196612
  188.2 21.7 %copy-start.4 = (f32[2,32]{1,0:T(2,128)S(1)}, f32[2,32]{1,0:T(2,128)}, u32[]{:S(2)}) copy-start(f32[2,32]{1,0:T(2,128)} %param.4) | copy-start | bytes 772
Sparse Core Ops, SparseCore 0:
  16.3 141.6 all-reduce.3
where the time goes:
time: 218 us; the launch traced here: 217 us
  waiting for transfers between devices  142 us (65%)
  other arithmetic  26.5 us (12%)
  matrix products  25.5 us (12%)
  between operations  14.2 us (7%)
  blocking collectives  4.89 us (2%)
  local copies, waits for them, and re-layouts  4.35 us (2%)
    psum x1, waiting for transfers between devices, shards(): projections = lax.psum(local_proj, 'tm')  142 us
    another operation x4, other arithmetic, factor_solve(): lax.linalg.triangular_solve(factor, lower_part, left_side=True, lower=Tru...  11.1 us
    dot_general x1, matrix products, shards(): jnp.dot(basis_b[:, :2 * modes], signed, preferred_element_type=jnp.float32)  9.2 us
    dot_general x1, matrix products, shards(): lax.dot_general(snapshots, basis_b, (((0,), (0,)), ((), ())), preferred_e...  6.77 us
    another operation x3, other arithmetic, basis_solve(): factor = jnp.linalg.cholesky(embedded(g_real, g_imag))  6.53 us
    another operation x3, other arithmetic, lm_update(): factor = jnp.linalg.cholesky(embedded(h_real, h_imag))  6.53 us
    psum x1, blocking collectives, shards(): self_terms, cross_sums = lax.psum((self_terms, cross_sums), 'space')  4.89 us
  transfers between devices with their start and end apart: 1, of which 1 were waited for; matrix products, arithmetic and copies ran while one was open for 0% of the time, Pallas kernels for 0%

commit v1 on v0

v1 whole, which is shorter than its diff:
```python
import jax
import jax.numpy as jnp
from jax import lax
from jax.experimental import pallas as pl
from jax.experimental.pallas import tpu as pltpu
from jax.sharding import PartitionSpec as P

damping = 0.01
MODES = 32
TIMES = 32768
ROWS = 512
COLS = 8192
QUARTER = COLS // 4
PART = QUARTER // 4
COARSE = 256
FINE = TIMES // COARSE
EXACT = lax.Precision.HIGHEST
VMEM = pl.BlockSpec(memory_space=pltpu.VMEM)
PARAMS = pltpu.CompilerParams(vmem_limit_bytes=48 * 1024 * 1024)


def place(device):
    return device >> 5, (device >> 3) & 3, (device >> 1) & 3, device & 1


def shifted(axis, step):
    pairs = []
    for device in range(128):
        z, y, x, core = place(device)
        along = "z" if axis == "z" else ("xy" if axis == "u" else "yx")[core]
        if along == "z":
            z = (z + step) % 4
        elif along == "y":
            y = (y + step) % 4
        else:
            x = (x + step) % 4
        pairs.append((device, ((z * 4 + y) * 4 + x) * 2 + core))
    return pairs


def send(value, axis, step):
    return lax.ppermute(value, ("tm", "space"), shifted(axis, step))


def swap_cores(value):
    return lax.ppermute(value, ("tm", "space"), [(d, d ^ 1) for d in range(128)])


def dot(left, right):
    return jnp.dot(left, right, precision=EXACT, preferred_element_type=jnp.float32)


def dot_t(left, right):
    return lax.dot_general(
        left, right, (((1,), (1,)), ((), ())), precision=EXACT, preferred_element_type=jnp.float32
    )


def waves(exponents, times):
    magnitude = jnp.exp(times[None, :] * exponents[0][:, None])
    phase_angle = times[None, :] * exponents[1][:, None]
    return magnitude * jnp.cos(phase_angle), magnitude * jnp.sin(phase_angle)


def table(exponents, times):
    real, imag = waves(exponents, times)
    both = jnp.concatenate([times, times])[None, :]
    plain = jnp.concatenate([real, imag], 1)
    turned = jnp.concatenate([imag, -real], 1)
    return jnp.stack([plain, turned, both * plain, both * turned])


def complex_product(a, b):
    return a[0] * b[0] - a[1] * b[1], a[0] * b[1] + a[1] * b[0]


def eliminate(real, imag, size):
    row_index = lax.broadcasted_iota(jnp.int32, real.shape, 0)
    for k in range(size):
        inverse_pivot = 1.0 / real[k : k + 1, k : k + 1]
        row_real = real[k : k + 1, :] * inverse_pivot
        row_imag = imag[k : k + 1, :] * inverse_pivot
        col_real = real[:, k : k + 1]
        col_imag = imag[:, k : k + 1]
        next_real = real - (col_real * row_real - col_imag * row_imag)
        next_imag = imag - (col_real * row_imag + col_imag * row_real)
        here = row_index == k
        real = jnp.where(here, row_real, next_real)
        imag = jnp.where(here, row_imag, next_imag)
    return real, imag


def grams(t):
    plain, turned, t_plain, t_turned = t[0], t[1], t[2], t[3]
    g = (dot_t(plain, plain), dot_t(plain, turned))
    c = (dot_t(plain, t_plain), dot_t(plain, t_turned))
    ct = (dot_t(t_plain, plain), dot_t(t_turned, plain))
    e = (dot_t(t_plain, t_plain), dot_t(t_plain, t_turned))
    gt = (dot_t(plain, plain), dot_t(turned, plain))
    return g, c, e, gt, ct


def add(a, b):
    return a[0] + b[0], a[1] + b[1]


def gram_kernel(coarse_ref, fine_ref, solve_ref, terms_ref):
    ga, ca, ea, gta, cta = grams(coarse_ref)
    gb, cb, eb, gtb, ctb = grams(fine_ref)
    g = complex_product(ga, gb)
    c = add(complex_product(ca, gb), complex_product(ga, cb))
    ct = add(complex_product(cta, gtb), complex_product(gta, ctb))
    cross = complex_product(ca, cb)
    e = add(complex_product(ea, gb), complex_product(ga, eb))
    e = (e[0] + 2.0 * cross[0], e[1] + 2.0 * cross[1])
    row = lax.broadcasted_iota(jnp.int32, (MODES, MODES), 0)
    col = lax.broadcasted_iota(jnp.int32, (MODES, MODES), 1)
    one = (row == col).astype(jnp.float32)
    real = jnp.concatenate([g[0], one], 1)
    imag = jnp.concatenate([g[1], jnp.zeros_like(one)], 1)
    real, imag = eliminate(real, imag, MODES)
    inv_real, inv_imag = real[:, MODES:], imag[:, MODES:]
    solve_ref[...] = jnp.concatenate(
        [jnp.concatenate([inv_real, inv_imag], 1), jnp.concatenate([inv_imag, -inv_real], 1)], 0
    )
    d_real = dot(inv_real, c[0]) - dot(inv_imag, c[1])
    d_imag = dot(inv_real, c[1]) + dot(inv_imag, c[0])
    terms_ref[0] = e[0] - (dot(ct[0], d_real) + dot(ct[1], d_imag))
    terms_ref[1] = e[1] - (dot(ct[0], d_imag) - dot(ct[1], d_real))
    terms_ref[2] = ct[0]
    terms_ref[3] = ct[1]


def project_kernel(index_ref, basis_ref, snapshots_ref, out_ref):
    out_ref[0] = jnp.dot(
        basis_ref[...], snapshots_ref[...], preferred_element_type=jnp.float32
    )


def project(index, basis_t, snapshots):
    return pl.pallas_call(
        project_kernel,
        grid_spec=pltpu.PrefetchScalarGridSpec(
            num_scalar_prefetch=1,
            grid=(4,),
            in_specs=[
                pl.BlockSpec((4 * MODES, ROWS), lambda j, i: (0, 0)),
                pl.BlockSpec((ROWS, PART), lambda j, i: (0, i[0] * 4 + j)),
            ],
            out_specs=pl.BlockSpec((1, 4 * MODES, PART), lambda j, i: (j, 0, 0)),
        ),
        out_shape=jax.ShapeDtypeStruct((4, 4 * MODES, PART), jnp.float32),
        compiler_params=PARAMS,
        cost_estimate=pl.CostEstimate(
            flops=2 * 128 * ROWS * QUARTER, bytes_accessed=3 << 20, transcendentals=0
        ),
        name="project",
    )(index, basis_t, snapshots)


def first_sum_kernel(v_ref, own_ref, r1_ref, r2_ref, r3_ref, *out_refs):
    for step in range(4):
        j = (v_ref[0] + step) & 3
        out_refs[step][...] = (own_ref[j] + r2_ref[j]) + (r1_ref[j] + r3_ref[j])


def first_sum(v, own, received):
    return pl.pallas_call(
        first_sum_kernel,
        in_specs=[pl.BlockSpec(memory_space=pltpu.SMEM)] + [VMEM] * 4,
        out_specs=[VMEM] * 4,
        out_shape=[jax.ShapeDtypeStruct((4 * MODES, PART), jnp.float32)] * 4,
        compiler_params=PARAMS,
        name="first_sum",
    )(v, own, *received)


def sum_kernel(own_ref, r1_ref, r2_ref, r3_ref, out_ref):
    out_ref[...] = (own_ref[...] + r2_ref[...]) + (r1_ref[...] + r3_ref[...])


def plain_sum(own, received):
    return pl.pallas_call(
        sum_kernel,
        in_specs=[VMEM] * 4,
        out_specs=VMEM,
        out_shape=jax.ShapeDtypeStruct(own.shape, jnp.float32),
        compiler_params=PARAMS,
        name="plain_sum",
    )(own, *received)


def amplitude_kernel(solve_ref, own_ref, r1_ref, r2_ref, r3_ref, out_ref):
    total = (own_ref[...] + r2_ref[...]) + (r1_ref[...] + r3_ref[...])
    amp = dot(solve_ref[...], total[: 2 * MODES])
    out_ref[:, :PART] = amp
    amp_real, amp_imag = amp[:MODES], amp[MODES:]
    z_cos, z_sin = total[2 * MODES : 3 * MODES], total[3 * MODES :]
    v_real = jnp.sum(amp_real * z_cos - amp_imag * z_sin, 1, keepdims=True)
    v_imag = jnp.sum(-amp_real * z_sin - amp_imag * z_cos, 1, keepdims=True)
    v = jnp.concatenate([v_real, v_imag], 0)
    s = dot_t(amp, amp)
    out_ref[:, PART:] = jnp.concatenate([s, jnp.broadcast_to(v, (64, 64))], 1)


def amplitudes_of(solve, own, received):
    return pl.pallas_call(
        amplitude_kernel,
        in_specs=[VMEM] * 5,
        out_specs=VMEM,
        out_shape=jax.ShapeDtypeStruct((2 * MODES, PART + 128), jnp.float32),
        compiler_params=PARAMS,
        name="amplitudes",
    )(solve, own, *received)


def join_kernel(v_ref, own_ref, r1_ref, r2_ref, r3_ref, out_ref):
    for step, ref in enumerate((own_ref, r1_ref, r2_ref, r3_ref)):
        j = (v_ref[0] - step) & 3
        out_ref[:, pl.ds(pl.multiple_of(j * PART, PART), PART)] = ref[:, :PART]
    out_ref[:, QUARTER:] = (own_ref[:, PART:] + r2_ref[:, PART:]) + (
        r1_ref[:, PART:] + r3_ref[:, PART:]
    )


def join(v, own, received):
    return pl.pallas_call(
        join_kernel,
        in_specs=[pl.BlockSpec(memory_space=pltpu.SMEM)] + [VMEM] * 4,
        out_specs=VMEM,
        out_shape=jax.ShapeDtypeStruct((2 * MODES, QUARTER + 128), jnp.float32),
        compiler_params=PARAMS,
        name="join",
    )(v, own, *received)


def residual_kernel(index_ref, basis_ref, amp_ref, snapshots_ref, *refs):
    residual_ref, amp_out_ref = refs[-2:]
    amp = amp_ref[...]
    amp_out_ref[...] = amp
    signed = jnp.concatenate([amp[:MODES], -amp[MODES:]], 0).astype(jnp.bfloat16)
    fitted = jnp.dot(basis_ref[...], signed, preferred_element_type=jnp.float32)
    residual_ref[...] = (snapshots_ref[...].astype(jnp.float32) - fitted).astype(jnp.bfloat16)


def residual_part(index, basis, amp, snapshots, before):
    kept = [] if before is None else list(before)
    return pl.pallas_call(
        residual_kernel,
        grid_spec=pltpu.PrefetchScalarGridSpec(
            num_scalar_prefetch=1,
            grid=(4,),
            in_specs=[
                pl.BlockSpec((ROWS, 2 * MODES), lambda j, i: (0, 0)),
                pl.BlockSpec((2 * MODES, PART), lambda j, i: (0, j)),
                pl.BlockSpec((ROWS, PART), lambda j, i: (0, i[0] * 4 + j)),
            ]
            + [pl.BlockSpec(memory_space=pl.ANY)] * len(kept),
            out_specs=[
                pl.BlockSpec((ROWS, PART), lambda j, i: (0, i[0] * 4 + j)),
                pl.BlockSpec((2 * MODES, PART), lambda j, i: (0, i[0] * 4 + j)),
            ],
        ),
        out_shape=[
            jax.ShapeDtypeStruct((ROWS, COLS), jnp.bfloat16),
            jax.ShapeDtypeStruct((2 * MODES, COLS), jnp.float32),
        ],
        input_output_aliases={4: 0, 5: 1} if kept else {},
        compiler_params=PARAMS,
        cost_estimate=pl.CostEstimate(
            flops=2 * 64 * ROWS * QUARTER, bytes_accessed=5 << 20, transcendentals=0
        ),
        name="residual_part",
    )(index, basis, amp, snapshots, *kept)


def update_kernel(exponents_ref, terms_ref, here_ref, there_ref, out_ref):
    total = here_ref[...] + there_ref[...]
    s_real = total[:MODES, :MODES] + total[MODES:, MODES : 2 * MODES]
    s_imag = total[:MODES, MODES : 2 * MODES] - total[MODES:, :MODES]
    v_real = total[:MODES, 2 * MODES : 2 * MODES + 1]
    v_imag = total[MODES:, 2 * MODES : 2 * MODES + 1]
    m_real, m_imag, ct_real, ct_imag = (terms_ref[i] for i in range(4))
    row = lax.broadcasted_iota(jnp.int32, (MODES, MODES), 0)
    col = lax.broadcasted_iota(jnp.int32, (MODES, MODES), 1)
    one = (row == col).astype(jnp.float32)
    w_real = jnp.sum(ct_real * s_real + ct_imag * s_imag, 1, keepdims=True)
    w_imag = jnp.sum(ct_real * s_imag - ct_imag * s_real, 1, keepdims=True)
    h_real = s_real * m_real - s_imag * m_imag + damping * one
    h_imag = s_real * m_imag + s_imag * m_real
    wide = (MODES, MODES)
    real = jnp.concatenate([h_real, jnp.broadcast_to(w_real - v_real, wide)], 1)
    imag = jnp.concatenate([h_imag, jnp.broadcast_to(w_imag - v_imag, wide)], 1)
    real, imag = eliminate(real, imag, MODES)
    step_real = jnp.sum(one * real[:, MODES:], 0, keepdims=True)
    step_imag = jnp.sum(one * imag[:, MODES:], 0, keepdims=True)
    out_ref[...] = exponents_ref[...] - jnp.concatenate([step_real, step_imag], 0)


def shards(snapshots, exponents):
    z, y, x, core = place(lax.axis_index("tm") * 2 + lax.axis_index("space"))
    u = jnp.where(core == 0, x, y).astype(jnp.int32)
    v = jnp.where(core == 0, y, x).astype(jnp.int32)
    at_v = v[None]
    first_row = lax.axis_index("tm") * ROWS
    times = (first_row + jnp.arange(ROWS, dtype=jnp.int32)).astype(jnp.float32) / TIMES
    real, imag = waves(exponents, times)
    basis_t = jnp.concatenate([real, imag], 0)
    basis_t = jnp.concatenate([basis_t, times[None, :] * basis_t], 0).astype(jnp.bfloat16)
    basis = basis_t[: 2 * MODES].T

    received = {}
    for step in (2, 1, 3):
        part = project(((u + step) & 3)[None], basis_t, snapshots)
        received[step] = send(part, "u", step)
    own = project(u[None], basis_t, snapshots)

    coarse = table(exponents, jnp.arange(COARSE, dtype=jnp.float32) / COARSE)
    fine = table(exponents, jnp.arange(FINE, dtype=jnp.float32) / TIMES)
    solve, terms = pl.pallas_call(
        gram_kernel,
        in_specs=[VMEM] * 2,
        out_specs=[VMEM] * 2,
        out_shape=[
            jax.ShapeDtypeStruct((2 * MODES, 2 * MODES), jnp.float32),
            jax.ShapeDtypeStruct((4, MODES, MODES), jnp.float32),
        ],
        compiler_params=PARAMS,
        cost_estimate=pl.CostEstimate(
            flops=1 << 30, bytes_accessed=16 << 20, transcendentals=0
        ),
        name="gram",
    )(coarse, fine)

    sums = first_sum(at_v, own, [received[s] for s in (1, 2, 3)])
    received = {s: send(sums[s], "v", s) for s in (2, 1, 3)}
    total = plain_sum(sums[0], [received[s] for s in (1, 2, 3)])
    received = {s: send(total, "z", s) for s in (2, 1, 3)}
    amp = amplitudes_of(solve, total, [received[s] for s in (1, 2, 3)])
    received = {s: send(amp, "v", s) for s in (2, 1, 3)}
    amp = join(at_v, amp, [received[s] for s in (1, 2, 3)])
    received = {s: send(amp, "u", s) for s in (2, 1, 3)}
    out = residual_part(u[None], basis, amp, snapshots, None)
    sums = plain_sum(
        amp[:, QUARTER:], [received[s][:, QUARTER:] for s in (1, 2, 3)]
    )
    other = swap_cores(sums)
    for step in (1, 3, 2):
        out = residual_part(((u - step) & 3)[None], basis, received[step], snapshots, out)
    residual, amp = out
    new_exponents = pl.pallas_call(
        update_kernel,
        in_specs=[VMEM] * 4,
        out_specs=VMEM,
        out_shape=jax.ShapeDtypeStruct((2, MODES), jnp.float32),
        compiler_params=PARAMS,
        name="update",
    )(exponents, terms, sums, other)
    return (new_exponents, amp.reshape(2, MODES, COLS), residual)


def solution(mesh):
    return jax.shard_map(
        shards,
        mesh=mesh,
        in_specs=(P("tm", "space"), P()),
        out_specs=(P(), P(None, None, "space"), P("tm", "space")),
        check_vma=False,
    )
```

time: 218 us -> 118 us (0.54)
  waiting for transfers between devices: 142 us -> 46.7 us
  Pallas kernels: 0 us -> 40.7 us
  starting transfers between devices: 0.04 us -> 26.5 us
  matrix products: 25.5 us -> 0 us
  other arithmetic: 26.5 us -> 1.94 us
  between operations: 14.2 us -> 0.81 us
  blocking collectives: 4.89 us -> 0 us
  local copies, waits for them, and re-layouts: 4.35 us -> 0.89 us
    psum x1 -> x0, waiting for transfers between devices: 142 us -> none  [shards(): projections = lax.psum(local_proj, 'tm')]
    ppermute x0 -> x16, waiting for transfers between devices: none -> 46.7 us  [the longest x15 46.7 us: send(): return lax.ppermute(value, ('tm', 'space'), shifted(axis, step))]
    pallas_call x0 -> x15, Pallas kernels: none -> 40.7 us  [the longest x4 17.3 us: residual_part(): pl.pallas_call(residual_kernel, grid_spec=pltpu.PrefetchScalarGridSpec(nu...]
    ppermute x0 -> x16, starting transfers between devices: none -> 26.5 us  [the longest x15 22.4 us: send(): return lax.ppermute(value, ('tm', 'space'), shifted(axis, step))]
    dot_general x8 -> x0, matrix products: 24.8 us -> none  [the longest x1 9.2 us: shards(): jnp.dot(basis_b[:, :2 * modes], signed, preferred_element_type=jnp.float32)]
    another operation x11 -> x6, other arithmetic: 24.2 us -> 1.3 us  [the longest x4 11.1 us: factor_solve(): lax.linalg.triangular_solve(factor, lower_part, left_side=True, lower=Tru...]
    psum x1 -> x0, blocking collectives: 4.89 us -> none  [shards(): self_terms, cross_sums = lax.psum((self_terms, cross_sums), 'space')]
    gather x4 -> x0, local copies, waits for them, and re-layouts: 3.04 us -> none  [the longest x1 0.9 us: fit_terms(): jnp.diagonal(cross[:modes, modes:]) - jnp.diagonal(cross[modes:, :modes])]
  transfers between devices with their start and end apart: 1 -> 16, of which waited for: 1 -> 12; matrix products, arithmetic and copies ran while one was open for 0% -> 0% of each run, Pallas kernels for 0% -> 27%
where the time goes in v1:
time: 118 us; the launch traced here: 117 us
  waiting for transfers between devices  46.7 us (40%)
  Pallas kernels  40.7 us (34%)
  starting transfers between devices  26.5 us (22%)
  other arithmetic  1.94 us (2%)
    ppermute x15, waiting for transfers between devices, send(): return lax.ppermute(value, ('tm', 'space'), shifted(axis, step))  46.7 us
    ppermute x15, starting transfers between devices, send(): return lax.ppermute(value, ('tm', 'space'), shifted(axis, step))  22.4 us
    pallas_call x4, Pallas kernels, residual_part(): pl.pallas_call(residual_kernel, grid_spec=pltpu.PrefetchScalarGridSpec(nu...  17.3 us
    pallas_call x4, Pallas kernels, project(): pl.pallas_call(project_kernel, grid_spec=pltpu.PrefetchScalarGridSpec(num...  13.7 us
    ppermute x1, starting transfers between devices, swap_cores(): lax.ppermute(value, ('tm', 'space'), [(d, d ^ 1) for d in range(128)])  4.1 us
    pallas_call x1, Pallas kernels, shards(): pl.pallas_call(gram_kernel, in_specs=[VMEM] * 2, out_specs=[VMEM] * 2, ou...  3.88 us
    pallas_call x1, Pallas kernels, shards(): pl.pallas_call(update_kernel, in_specs=[VMEM] * 4, out_specs=VMEM, out_sh...  3.73 us
  transfers between devices with their start and end apart: 16, of which 12 were waited for; matrix products, arithmetic and copies ran while one was open for 0% of the time, Pallas kernels for 27%

profile of v1, /device:TPU:1, one launch (start us, length us, event | category | flops | bytes accessed | tf_op | source)
XLA Modules:
  0.0 117.5 jit_solution(9079213390969469233)
XLA Ops:
  2.9 2.9 %project.5 = f32[4,128,512]{2,1,0:T(8,128)S(1)} custom-call(s32[1]{0:T(128)} %bitcast.14.index_ref, bf16[128,512]{1,0:T(8,128)(2,1)S(1)} %copy.17.basis_ref, bf16[512,8192]{1,0:T(8,128)(2,1)} %snapshots_ref.15), custom_call_target="tpu_custom_call" | custom-call | flops 268435456 | bytes 3145728 | tf_op jit(solution)/shard_map/project/pallas_call | solution.py:141
  5.8 2.2 %collective-permute-start = (f32[4,128,512]{2,1,0:T(8,128)S(1)}, f32[4,128,512]{2,1,0:T(8,128)S(1)}, u32[]{:S(2)}, u32[]{:S(2)}) collective-permute-start(f32[4,128,512]{2,1,0:T(8,128)S(1)} %project.5), channel_id=1, source_target_pairs={{0,2},{1,9},{2,4},{3,11},{4,6},{5,13},{6,0},{7,15},{8,10},{9,17},{... | collective-permute-start | bytes 3145736 | tf_op jit(solution)/shard_map/ppermute | solution.py:42
  8.0 4.0 %project.6 = f32[4,128,512]{2,1,0:T(8,128)} custom-call(s32[1]{0:T(128)} %bitcast.15.index_ref, bf16[128,512]{1,0:T(8,128)(2,1)S(1)} %copy.17.basis_ref, bf16[512,8192]{1,0:T(8,128)(2,1)} %snapshots_ref.15), custom_call_target="tpu_custom_call" | custom-call | flops 268435456 | bytes 3145728 | tf_op jit(solution)/shard_map/project/pallas_call | solution.py:141
  12.0 2.6 %collective-permute-start.1 = (f32[4,128,512]{2,1,0:T(8,128)}, f32[4,128,512]{2,1,0:T(8,128)S(1)}, u32[]{:S(2)}, u32[]{:S(2)}) collective-permute-start(f32[4,128,512]{2,1,0:T(8,128)} %project.6), channel_id=1, source_target_pairs={{0,4},{1,17},{2,6},{3,19},{4,0},{5,21},{6,2},{7,23},{8,12},{9,25},... | collective-permute-start | bytes 3145736 | tf_op jit(solution)/shard_map/ppermute | solution.py:42
  14.6 4.0 %project.7 = f32[4,128,512]{2,1,0:T(8,128)} custom-call(s32[1]{0:T(128)} %bitcast.16.index_ref, bf16[128,512]{1,0:T(8,128)(2,1)S(1)} %copy.17.basis_ref, bf16[512,8192]{1,0:T(8,128)(2,1)} %snapshots_ref.15), custom_call_target="tpu_custom_call" | custom-call | flops 268435456 | bytes 3145728 | tf_op jit(solution)/shard_map/project/pallas_call | solution.py:141
  19.7 2.9 %project.4.own_ref = f32[4,128,512]{2,1,0:T(8,128)S(1)} custom-call(s32[1]{0:T(128)} %bitcast.13.index_ref, bf16[128,512]{1,0:T(8,128)(2,1)S(1)} %copy.17.basis_ref, bf16[512,8192]{1,0:T(8,128)(2,1)} %snapshots_ref.15), custom_call_target="tpu_custom_call" | custom-call | flops 268435456 | bytes 3145728 | tf_op jit(solution)/shard_map/project/pallas_call | solution.py:141
  23.0 11.4 %collective-permute-done.1.r2_ref = f32[4,128,512]{2,1,0:T(8,128)S(1)} collective-permute-done((f32[4,128,512]{2,1,0:T(8,128)}, f32[4,128,512]{2,1,0:T(8,128)S(1)}, u32[]{:S(2)}, u32[]{:S(2)}) %collective-permute-start.1) | collective-permute-done | bytes 1048608 | tf_op jit(solution)/shard_map/ppermute | solution.py:42
  34.3 3.8 %collective-permute-done.2.r3_ref = f32[4,128,512]{2,1,0:T(8,128)} collective-permute-done((f32[4,128,512]{2,1,0:T(8,128)}, f32[4,128,512]{2,1,0:T(8,128)}, u32[]{:S(2)}, u32[]{:S(2)}) %collective-permute-start.2) | collective-permute-done | bytes 1048608 | tf_op jit(solution)/shard_map/ppermute | solution.py:42
  38.1 1.4 %first_sum.1 = (f32[128,512]{1,0:T(8,128)S(1)}, f32[128,512]{1,0:T(8,128)S(1)}, f32[128,512]{1,0:T(8,128)S(1)}, f32[128,512]{1,0:T(8,128)S(1)}) custom-call(s32[1]{0:T(128)} %bitcast.12.v_ref, f32[4,128,512]{2,1,0:T(8,128)S(1)} %project.4.own_ref, f32[4,128,512]{2,1,0:T(8,128)S(1)} %collective-permute-done.r1_ref, ...), custom_call_target="tpu_custom_call" | custom-call | tf_op jit(solution)/shard_map/first_sum/pallas_call | solution.py:168
  39.5 1.3 %collective-permute-start.3 = (f32[128,512]{1,0:T(8,128)S(1)}, f32[128,512]{1,0:T(8,128)S(1)}, u32[]{:S(2)}, u32[]{:S(2)}) collective-permute-start(f32[128,512]{1,0:T(8,128)S(1)} %get-tuple-element.20), channel_id=1, source_target_pairs={{0,8},{1,3},{2,10},{3,5},{4,12},{5,7},{6,14},{7,1},{8,16},{9,11},{... | collective-permute-start | bytes 786440 | tf_op jit(solution)/shard_map/ppermute | solution.py:42
  40.8 2.5 %collective-permute-start.4 = (f32[128,512]{1,0:T(8,128)S(1)}, f32[128,512]{1,0:T(8,128)S(1)}, u32[]{:S(2)}, u32[]{:S(2)}) collective-permute-start(f32[128,512]{1,0:T(8,128)S(1)} %get-tuple-element.21), channel_id=1, source_target_pairs={{0,16},{1,5},{2,18},{3,7},{4,20},{5,1},{6,22},{7,3},{8,24},{9,13},... | collective-permute-start | bytes 786440 | tf_op jit(solution)/shard_map/ppermute | solution.py:42
  43.3 1.2 collective-permute-start.5
  44.4 1.9 %collective-permute-done.3.r1_ref = f32[128,512]{1,0:T(8,128)S(1)} collective-permute-done((f32[128,512]{1,0:T(8,128)S(1)}, f32[128,512]{1,0:T(8,128)S(1)}, u32[]{:S(2)}, u32[]{:S(2)}) %collective-permute-start.3) | collective-permute-done | bytes 262176 | tf_op jit(solution)/shard_map/ppermute | solution.py:42
  46.3 3.8 %collective-permute-done.4.r2_ref = f32[128,512]{1,0:T(8,128)S(1)} collective-permute-done((f32[128,512]{1,0:T(8,128)S(1)}, f32[128,512]{1,0:T(8,128)S(1)}, u32[]{:S(2)}, u32[]{:S(2)}) %collective-permute-start.4) | collective-permute-done | bytes 262176 | tf_op jit(solution)/shard_map/ppermute | solution.py:42
  50.2 3.8 %collective-permute-start.8 = (f32[128,512]{1,0:T(8,128)S(1)}, f32[128,512]{1,0:T(8,128)S(1)}, u32[]{:S(2)}, u32[]{:S(2)}) collective-permute-start(f32[128,512]{1,0:T(8,128)S(1)} %plain_sum.2.own_ref), channel_id=1, source_target_pairs={{0,96},{1,97},{2,98},{3,99},{4,100},{5,101},{6,102},{7,103},{8,104... | collective-permute-start | bytes 786440 | tf_op jit(solution)/shard_map/ppermute | solution.py:42
  54.8 3.9 %gram.1 = (f32[64,64]{1,0:T(8,128)S(1)}, f32[4,32,32]{2,1,0:T(8,128)S(1)}) custom-call(f32[4,32,512]{2,1,0:T(8,128)S(1)} %pad_maximum_fusion.coarse_ref, f32[4,32,256]{2,1,0:T(8,128)S(1)} %pad_maximum_fusion.1.fine_ref), custom_call_target="tpu_custom_call" | custom-call | flops 1073741824 | bytes 16777216 | tf_op jit(solution)/shard_map/gram/pallas_call | solution.py:320
  58.6 5.2 %collective-permute-done.8.r3_ref = f32[128,512]{1,0:T(8,128)S(1)} collective-permute-done((f32[128,512]{1,0:T(8,128)S(1)}, f32[128,512]{1,0:T(8,128)S(1)}, u32[]{:S(2)}, u32[]{:S(2)}) %collective-permute-start.8) | collective-permute-done | bytes 262176 | tf_op jit(solution)/shard_map/ppermute | solution.py:42
  63.8 4.5 %collective-permute-done.6.r1_ref = f32[128,512]{1,0:T(8,128)S(1)} collective-permute-done((f32[128,512]{1,0:T(8,128)S(1)}, f32[128,512]{1,0:T(8,128)S(1)}, u32[]{:S(2)}, u32[]{:S(2)}) %collective-permute-start.6) | collective-permute-done | bytes 262176 | tf_op jit(solution)/shard_map/ppermute | solution.py:42
  68.9 1.7 %collective-permute-start.11 = (f32[64,640]{1,0:T(8,128)S(1)}, f32[64,640]{1,0:T(8,128)S(1)}, u32[]{:S(2)}, u32[]{:S(2)}) collective-permute-start(f32[64,640]{1,0:T(8,128)S(1)} %amplitudes.1.own_ref), channel_id=1, source_target_pairs={{0,24},{1,7},{2,26},{3,1},{4,28},{5,3},{6,30},{7,5},{8,0},{9,15},{... | collective-permute-start | bytes 491528 | tf_op jit(solution)/shard_map/ppermute | solution.py:42
  71.9 2.8 %collective-permute-done.11.r3_ref = f32[64,640]{1,0:T(8,128)S(1)} collective-permute-done((f32[64,640]{1,0:T(8,128)S(1)}, f32[64,640]{1,0:T(8,128)S(1)}, u32[]{:S(2)}, u32[]{:S(2)}) %collective-permute-start.11) | collective-permute-done | bytes 163872 | tf_op jit(solution)/shard_map/ppermute | solution.py:42
  74.6 1.8 %collective-permute-done.10.r2_ref = f32[64,640]{1,0:T(8,128)S(1)} collective-permute-done((f32[64,640]{1,0:T(8,128)S(1)}, f32[64,640]{1,0:T(8,128)S(1)}, u32[]{:S(2)}, u32[]{:S(2)}) %collective-permute-start.10) | collective-permute-done | bytes 163872 | tf_op jit(solution)/shard_map/ppermute | solution.py:42
  76.4 1.9 %collective-permute-done.9.r1_ref = f32[64,640]{1,0:T(8,128)S(1)} collective-permute-done((f32[64,640]{1,0:T(8,128)S(1)}, f32[64,640]{1,0:T(8,128)S(1)}, u32[]{:S(2)}, u32[]{:S(2)}) %collective-permute-start.9) | collective-permute-done | bytes 163872 | tf_op jit(solution)/shard_map/ppermute | solution.py:42
  78.4 2.2 %collective-permute-start.14 = (f32[64,2176]{1,0:T(8,128)S(1)}, f32[64,2176]{1,0:T(8,128)S(1)}, u32[]{:S(2)}, u32[]{:S(2)}) collective-permute-start(f32[64,2176]{1,0:T(8,128)S(1)} %join.1.amp_ref), channel_id=1, source_target_pairs={{0,6},{1,25},{2,0},{3,27},{4,2},{5,29},{6,4},{7,31},{8,14},{9,1},{... | collective-permute-start | bytes 1671176 | tf_op jit(solution)/shard_map/ppermute | solution.py:42
  80.5 2.0 %collective-permute-start.13 = (f32[64,2176]{1,0:T(8,128)S(1)}, f32[64,2176]{1,0:T(8,128)S(1)}, u32[]{:S(2)}, u32[]{:S(2)}) collective-permute-start(f32[64,2176]{1,0:T(8,128)S(1)} %join.1.amp_ref), channel_id=1, source_target_pairs={{0,4},{1,17},{2,6},{3,19},{4,0},{5,21},{6,2},{7,23},{8,12},{9,25},... | collective-permute-start | bytes 1671176 | tf_op jit(solution)/shard_map/ppermute | solution.py:42
  82.6 4.4 %residual_part.4 = (bf16[512,8192]{1,0:T(8,128)(2,1)}, f32[64,8192]{1,0:T(8,128)}) custom-call(s32[1]{0:T(128)} %bitcast.13.index_ref, bf16[512,64]{1,0:T(8,128)(2,1)S(1)} %maximum_bitcast_fusion.basis_ref, f32[64,2176]{1,0:T(8,128)S(1)} %join.1.amp_ref, bf16[512,8192]{1,0:T(8,128)(2,1)} %snapshots_ref.15), custom_call_target="tpu_custom_call" | custom-call | flops 134217728 | bytes 5242880 | tf_op jit(solution)/shard_map/residual_part/pallas_call | solution.py:248
  87.9 2.8 %collective-permute-done.13.amp_ref = f32[64,2176]{1,0:T(8,128)S(1)} collective-permute-done((f32[64,2176]{1,0:T(8,128)S(1)}, f32[64,2176]{1,0:T(8,128)S(1)}, u32[]{:S(2)}, u32[]{:S(2)}) %collective-permute-start.13) | collective-permute-done | bytes 557088 | tf_op jit(solution)/shard_map/ppermute | solution.py:42
  90.8 5.9 %collective-permute-done.12.amp_ref = f32[64,2176]{1,0:T(8,128)S(1)} collective-permute-done((f32[64,2176]{1,0:T(8,128)S(1)}, f32[64,2176]{1,0:T(8,128)S(1)}, u32[]{:S(2)}, u32[]{:S(2)}) %collective-permute-start.12) | collective-permute-done | bytes 557088 | tf_op jit(solution)/shard_map/ppermute | solution.py:42
  96.7 4.1 %collective-permute-start.15 = (f32[64,128]{1,0:T(8,128)S(1)}, f32[64,128]{1,0:T(8,128)S(1)}, u32[]{:S(2)}, u32[]{:S(2)}) collective-permute-start(f32[64,128]{1,0:T(8,128)S(1)} %plain_sum.3.here_ref), channel_id=1, source_target_pairs={{0,1},{1,0},{2,3},{3,2},{4,5},{5,4},{6,7},{7,6},{8,9},{9,8},{10,11... | collective-permute-start | bytes 98312 | tf_op jit(solution)/shard_map/ppermute | solution.py:46
  100.8 4.3 %residual_part.5 = (bf16[512,8192]{1,0:T(8,128)(2,1)}, f32[64,8192]{1,0:T(8,128)}) custom-call(s32[1]{0:T(128)} %bitcast.20.index_ref, bf16[512,64]{1,0:T(8,128)(2,1)S(1)} %maximum_bitcast_fusion.basis_ref, f32[64,2176]{1,0:T(8,128)S(1)} %collective-permute-done.12.amp_ref, ...), custom_call_target="tpu_custom_call", output_to_operand_aliasing={{0}: (4, {}), {1}: (5, {})} | custom-call | flops 134217728 | bytes 5242880 | tf_op jit(solution)/shard_map/residual_part/pallas_call | solution.py:248
  105.1 4.3 %residual_part.6 = (bf16[512,8192]{1,0:T(8,128)(2,1)}, f32[64,8192]{1,0:T(8,128)}) custom-call(s32[1]{0:T(128)} %bitcast.19.index_ref, bf16[512,64]{1,0:T(8,128)(2,1)S(1)} %maximum_bitcast_fusion.basis_ref, f32[64,2176]{1,0:T(8,128)S(1)} %collective-permute-done.14.amp_ref, ...), custom_call_target="tpu_custom_call", output_to_operand_aliasing={{0}: (4, {}), {1}: (5, {})} | custom-call | flops 134217728 | bytes 5242880 | tf_op jit(solution)/shard_map/residual_part/pallas_call | solution.py:248
  109.4 4.4 %residual_part.7 = (bf16[512,8192]{1,0:T(8,128)(2,1)}, f32[64,8192]{1,0:T(8,128)}) custom-call(s32[1]{0:T(128)} %bitcast.17.index_ref, bf16[512,64]{1,0:T(8,128)(2,1)S(1)} %maximum_bitcast_fusion.basis_ref, f32[64,2176]{1,0:T(8,128)S(1)} %collective-permute-done.13.amp_ref, ...), custom_call_target="tpu_custom_call", output_to_operand_aliasing={{0}: (4, {}), {1}: (5, {})} | custom-call | flops 134217728 | bytes 5242880 | tf_op jit(solution)/shard_map/residual_part/pallas_call | solution.py:248
  113.8 3.7 %update.1 = f32[2,32]{1,0:T(2,128)} custom-call(f32[2,32]{1,0:T(2,128)S(1)} %copy-done, f32[4,32,32]{2,1,0:T(8,128)S(1)} %get-tuple-element.17.terms_ref, f32[64,128]{1,0:T(8,128)S(1)} %plain_sum.3.here_ref, f32[64,128]{1,0:T(8,128)S(1)} %collective-permute-done.15.there_ref), custom_call_target="tpu_custom_call" | custom-call | tf_op jit(solution)/shard_map/update/pallas_call | solution.py:351
  (40 shorter events, 7.5 us)
Async XLA Ops:
  5.8 17.2 %collective-permute-start = (f32[4,128,512]{2,1,0:T(8,128)S(1)}, f32[4,128,512]{2,1,0:T(8,128)S(1)}, u32[]{:S(2)}, u32[]{:S(2)}) collective-permute-start(f32[4,128,512]{2,1,0:T(8,128)S(1)} %project.5), channel_id=1, source_target_pairs={{0,2},{1,9},{2,4},{3,11},{4,6},{5,13},{6,0},{7,15},{8,10},{9,17},{... | collective-permute-start | bytes 3145736 | tf_op jit(solution)/shard_map/ppermute | solution.py:42
  12.0 22.3 %collective-permute-start.1 = (f32[4,128,512]{2,1,0:T(8,128)}, f32[4,128,512]{2,1,0:T(8,128)S(1)}, u32[]{:S(2)}, u32[]{:S(2)}) collective-permute-start(f32[4,128,512]{2,1,0:T(8,128)} %project.6), channel_id=1, source_target_pairs={{0,4},{1,17},{2,6},{3,19},{4,0},{5,21},{6,2},{7,23},{8,12},{9,25},... | collective-permute-start | bytes 3145736 | tf_op jit(solution)/shard_map/ppermute | solution.py:42
  18.6 19.5 %collective-permute-start.2 = (f32[4,128,512]{2,1,0:T(8,128)}, f32[4,128,512]{2,1,0:T(8,128)}, u32[]{:S(2)}, u32[]{:S(2)}) collective-permute-start(f32[4,128,512]{2,1,0:T(8,128)} %project.7), channel_id=1, source_target_pairs={{0,6},{1,25},{2,0},{3,27},{4,2},{5,29},{6,4},{7,31},{8,14},{9,1},{... | collective-permute-start | bytes 3145736 | tf_op jit(solution)/shard_map/ppermute | solution.py:42
  39.5 6.8 %collective-permute-start.3 = (f32[128,512]{1,0:T(8,128)S(1)}, f32[128,512]{1,0:T(8,128)S(1)}, u32[]{:S(2)}, u32[]{:S(2)}) collective-permute-start(f32[128,512]{1,0:T(8,128)S(1)} %get-tuple-element.20), channel_id=1, source_target_pairs={{0,8},{1,3},{2,10},{3,5},{4,12},{5,7},{6,14},{7,1},{8,16},{9,11},{... | collective-permute-start | bytes 786440 | tf_op jit(solution)/shard_map/ppermute | solution.py:42
  40.8 9.3 %collective-permute-start.4 = (f32[128,512]{1,0:T(8,128)S(1)}, f32[128,512]{1,0:T(8,128)S(1)}, u32[]{:S(2)}, u32[]{:S(2)}) collective-permute-start(f32[128,512]{1,0:T(8,128)S(1)} %get-tuple-element.21), channel_id=1, source_target_pairs={{0,16},{1,5},{2,18},{3,7},{4,20},{5,1},{6,22},{7,3},{8,24},{9,13},... | collective-permute-start | bytes 786440 | tf_op jit(solution)/shard_map/ppermute | solution.py:42
  43.3 6.9 %collective-permute-start.5 = (f32[128,512]{1,0:T(8,128)S(1)}, f32[128,512]{1,0:T(8,128)S(1)}, u32[]{:S(2)}, u32[]{:S(2)}) collective-permute-start(f32[128,512]{1,0:T(8,128)S(1)} %get-tuple-element.22), channel_id=1, source_target_pairs={{0,24},{1,7},{2,26},{3,1},{4,28},{5,3},{6,30},{7,5},{8,0},{9,15},{... | collective-permute-start | bytes 786440 | tf_op jit(solution)/shard_map/ppermute | solution.py:42
  50.2 13.7 %collective-permute-start.8 = (f32[128,512]{1,0:T(8,128)S(1)}, f32[128,512]{1,0:T(8,128)S(1)}, u32[]{:S(2)}, u32[]{:S(2)}) collective-permute-start(f32[128,512]{1,0:T(8,128)S(1)} %plain_sum.2.own_ref), channel_id=1, source_target_pairs={{0,96},{1,97},{2,98},{3,99},{4,100},{5,101},{6,102},{7,103},{8,104... | collective-permute-start | bytes 786440 | tf_op jit(solution)/shard_map/ppermute | solution.py:42
  54.0 9.8 %collective-permute-start.7 = (f32[128,512]{1,0:T(8,128)S(1)}, f32[128,512]{1,0:T(8,128)S(1)}, u32[]{:S(2)}, u32[]{:S(2)}) collective-permute-start(f32[128,512]{1,0:T(8,128)S(1)} %plain_sum.2.own_ref), channel_id=1, source_target_pairs={{0,64},{1,65},{2,66},{3,67},{4,68},{5,69},{6,70},{7,71},{8,72},{9,... | collective-permute-start | bytes 786440 | tf_op jit(solution)/shard_map/ppermute | solution.py:42
  54.0 14.3 %collective-permute-start.6 = (f32[128,512]{1,0:T(8,128)S(1)}, f32[128,512]{1,0:T(8,128)S(1)}, u32[]{:S(2)}, u32[]{:S(2)}) collective-permute-start(f32[128,512]{1,0:T(8,128)S(1)} %plain_sum.2.own_ref), channel_id=1, source_target_pairs={{0,32},{1,33},{2,34},{3,35},{4,36},{5,37},{6,38},{7,39},{8,40},{9,... | collective-permute-start | bytes 786440 | tf_op jit(solution)/shard_map/ppermute | solution.py:42
  68.9 5.7 %collective-permute-start.11 = (f32[64,640]{1,0:T(8,128)S(1)}, f32[64,640]{1,0:T(8,128)S(1)}, u32[]{:S(2)}, u32[]{:S(2)}) collective-permute-start(f32[64,640]{1,0:T(8,128)S(1)} %amplitudes.1.own_ref), channel_id=1, source_target_pairs={{0,24},{1,7},{2,26},{3,1},{4,28},{5,3},{6,30},{7,5},{8,0},{9,15},{... | collective-permute-start | bytes 491528 | tf_op jit(solution)/shard_map/ppermute | solution.py:42
  70.6 5.8 %collective-permute-start.10 = (f32[64,640]{1,0:T(8,128)S(1)}, f32[64,640]{1,0:T(8,128)S(1)}, u32[]{:S(2)}, u32[]{:S(2)}) collective-permute-start(f32[64,640]{1,0:T(8,128)S(1)} %amplitudes.1.own_ref), channel_id=1, source_target_pairs={{0,16},{1,5},{2,18},{3,7},{4,20},{5,1},{6,22},{7,3},{8,24},{9,13},... | collective-permute-start | bytes 491528 | tf_op jit(solution)/shard_map/ppermute | solution.py:42
  71.1 7.2 %collective-permute-start.9 = (f32[64,640]{1,0:T(8,128)S(1)}, f32[64,640]{1,0:T(8,128)S(1)}, u32[]{:S(2)}, u32[]{:S(2)}) collective-permute-start(f32[64,640]{1,0:T(8,128)S(1)} %amplitudes.1.own_ref), channel_id=1, source_target_pairs={{0,8},{1,3},{2,10},{3,5},{4,12},{5,7},{6,14},{7,1},{8,16},{9,11},{... | collective-permute-start | bytes 491528 | tf_op jit(solution)/shard_map/ppermute | solution.py:42
  78.4 9.6 %collective-permute-start.14 = (f32[64,2176]{1,0:T(8,128)S(1)}, f32[64,2176]{1,0:T(8,128)S(1)}, u32[]{:S(2)}, u32[]{:S(2)}) collective-permute-start(f32[64,2176]{1,0:T(8,128)S(1)} %join.1.amp_ref), channel_id=1, source_target_pairs={{0,6},{1,25},{2,0},{3,27},{4,2},{5,29},{6,4},{7,31},{8,14},{9,1},{... | collective-permute-start | bytes 1671176 | tf_op jit(solution)/shard_map/ppermute | solution.py:42
  80.5 10.2 %collective-permute-start.13 = (f32[64,2176]{1,0:T(8,128)S(1)}, f32[64,2176]{1,0:T(8,128)S(1)}, u32[]{:S(2)}, u32[]{:S(2)}) collective-permute-start(f32[64,2176]{1,0:T(8,128)S(1)} %join.1.amp_ref), channel_id=1, source_target_pairs={{0,4},{1,17},{2,6},{3,19},{4,0},{5,21},{6,2},{7,23},{8,12},{9,25},... | collective-permute-start | bytes 1671176 | tf_op jit(solution)/shard_map/ppermute | solution.py:42
  82.5 14.2 %collective-permute-start.12 = (f32[64,2176]{1,0:T(8,128)S(1)}, f32[64,2176]{1,0:T(8,128)S(1)}, u32[]{:S(2)}, u32[]{:S(2)}) collective-permute-start(f32[64,2176]{1,0:T(8,128)S(1)} %join.1.amp_ref), channel_id=1, source_target_pairs={{0,2},{1,9},{2,4},{3,11},{4,6},{5,13},{6,0},{7,15},{8,10},{9,17},{... | collective-permute-start | bytes 1671176 | tf_op jit(solution)/shard_map/ppermute | solution.py:42
  96.7 17.1 %collective-permute-start.15 = (f32[64,128]{1,0:T(8,128)S(1)}, f32[64,128]{1,0:T(8,128)S(1)}, u32[]{:S(2)}, u32[]{:S(2)}) collective-permute-start(f32[64,128]{1,0:T(8,128)S(1)} %plain_sum.3.here_ref), channel_id=1, source_target_pairs={{0,1},{1,0},{2,3},{3,2},{4,5},{5,4},{6,7},{7,6},{8,9},{9,8},{10,11... | collective-permute-start | bytes 98312 | tf_op jit(solution)/shard_map/ppermute | solution.py:46
  109.4 4.4 %copy-start = (f32[2,32]{1,0:T(2,128)S(1)}, f32[2,32]{1,0:T(2,128)}, u32[]{:S(2)}) copy-start(f32[2,32]{1,0:T(2,128)} %exponents_ref.1) | copy-start | bytes 772

commit v2 on v1

--- a/solution.py
+++ b/solution.py
@@ -12,11 +12,15 @@
 COLS = 8192
 QUARTER = COLS // 4
 PART = QUARTER // 4
+WIDTH = 512
+ORDER = (1, 3, 2)
 COARSE = 256
 FINE = TIMES // COARSE
 EXACT = lax.Precision.HIGHEST
 VMEM = pl.BlockSpec(memory_space=pltpu.VMEM)
-PARAMS = pltpu.CompilerParams(vmem_limit_bytes=48 * 1024 * 1024)
+PARAMS = pltpu.CompilerParams(vmem_limit_bytes=24 * 1024 * 1024)
+WIDE_PARAMS = pltpu.CompilerParams(vmem_limit_bytes=52 * 1024 * 1024)
+AXES = {"u": "xy", "v": "yz", "w": "zx"}
 
 
 def place(device):
@@ -27,7 +31,7 @@
     pairs = []
     for device in range(128):
         z, y, x, core = place(device)
-        along = "z" if axis == "z" else ("xy" if axis == "u" else "yx")[core]
+        along = AXES[axis][core]
         if along == "z":
             z = (z + step) % 4
         elif along == "y":
@@ -60,6 +64,37 @@
     magnitude = jnp.exp(times[None, :] * exponents[0][:, None])
     phase_angle = times[None, :] * exponents[1][:, None]
     return magnitude * jnp.cos(phase_angle), magnitude * jnp.sin(phase_angle)
+
+
+def basis_kernel(first_ref, exponents_ref, flat_ref, tall_ref):
+    row = lax.broadcasted_iota(jnp.int32, (MODES, MODES), 0)
+    col = lax.broadcasted_iota(jnp.int32, (MODES, MODES), 1)
+    values = exponents_ref[...]
+    rate = jnp.sum(jnp.where(row == col, values[0:1], 0.0), 1, keepdims=True)
+    frequency = jnp.sum(jnp.where(row == col, values[1:2], 0.0), 1, keepdims=True)
+    step = first_ref[0] + lax.broadcasted_iota(jnp.int32, (MODES, ROWS), 1)
+    times = step.astype(jnp.float32) * (1.0 / TIMES)
+    magnitude = jnp.exp(times * rate)
+    phase_angle = times * frequency
+    real = magnitude * jnp.cos(phase_angle)
+    imag = magnitude * jnp.sin(phase_angle)
+    plain = jnp.concatenate([real, imag], 0)
+    flat_ref[...] = jnp.concatenate([plain, times * real, times * imag], 0).astype(jnp.bfloat16)
+    tall_ref[...] = plain.T.astype(jnp.bfloat16)
+
+
+def make_basis(first_row, exponents):
+    return pl.pallas_call(
+        basis_kernel,
+        in_specs=[pl.BlockSpec(memory_space=pltpu.SMEM), VMEM],
+        out_specs=[VMEM] * 2,
+        out_shape=[
+            jax.ShapeDtypeStruct((4 * MODES, ROWS), jnp.bfloat16),
+            jax.ShapeDtypeStruct((ROWS, 2 * MODES), jnp.bfloat16),
+        ],
+        compiler_params=PARAMS,
+        name="basis",
+    )(first_row.astype(jnp.int32), exponents)
 
 
 def table(exponents, times):
@@ -131,31 +166,40 @@
     terms_ref[3] = ct[1]
 
 
-def project_kernel(index_ref, basis_ref, snapshots_ref, out_ref):
-    out_ref[0] = jnp.dot(
-        basis_ref[...], snapshots_ref[...], preferred_element_type=jnp.float32
-    )
-
-
-def project(index, basis_t, snapshots):
+def project_kernel(index_ref, basis_ref, snapshots_ref, *out_refs):
+    for step, out_ref in enumerate(out_refs):
+
+        @pl.when(pl.program_id(0) == step)
+        def _():
+            found = jnp.dot(
+                basis_ref[...], snapshots_ref[...], preferred_element_type=jnp.float32
+            )
+            for j in range(4):
+                out_ref[j] = found[:, j * PART : (j + 1) * PART]
+
+
+def project(indices, basis_t, snapshots):
+    count = indices.shape[0]
     return pl.pallas_call(
         project_kernel,
         grid_spec=pltpu.PrefetchScalarGridSpec(
             num_scalar_prefetch=1,
-            grid=(4,),
+            grid=(count,),
             in_specs=[
                 pl.BlockSpec((4 * MODES, ROWS), lambda j, i: (0, 0)),
-                pl.BlockSpec((ROWS, PART), lambda j, i: (0, i[0] * 4 + j)),
+                pl.BlockSpec((ROWS, QUARTER), lambda j, i: (0, i[j])),
             ],
-            out_specs=pl.BlockSpec((1, 4 * MODES, PART), lambda j, i: (j, 0, 0)),
+            out_specs=[pl.BlockSpec((4, 4 * MODES, PART), lambda j, i: (0, 0, 0))] * count,
         ),
-        out_shape=jax.ShapeDtypeStruct((4, 4 * MODES, PART), jnp.float32),
-        compiler_params=PARAMS,
+        out_shape=[jax.ShapeDtypeStruct((4, 4 * MODES, PART), jnp.float32)] * count,
+        compiler_params=WIDE_PARAMS,
         cost_estimate=pl.CostEstimate(
-            flops=2 * 128 * ROWS * QUARTER, bytes_accessed=3 << 20, transcendentals=0
+            flops=count * 2 * 128 * ROWS * QUARTER,
+            bytes_accessed=count * (3 << 20),
+            transcendentals=0,
         ),
         name="project",
-    )(index, basis_t, snapshots)
+    )(indices, basis_t, snapshots)
 
 
 def first_sum_kernel(v_ref, own_ref, r1_ref, r2_ref, r3_ref, *out_refs):
@@ -234,44 +278,111 @@
     )(v, own, *received)
 
 
-def residual_kernel(index_ref, basis_ref, amp_ref, snapshots_ref, *refs):
-    residual_ref, amp_out_ref = refs[-2:]
-    amp = amp_ref[...]
-    amp_out_ref[...] = amp
-    signed = jnp.concatenate([amp[:MODES], -amp[MODES:]], 0).astype(jnp.bfloat16)
-    fitted = jnp.dot(basis_ref[...], signed, preferred_element_type=jnp.float32)
-    residual_ref[...] = (snapshots_ref[...].astype(jnp.float32) - fitted).astype(jnp.bfloat16)
-
-
-def residual_part(index, basis, amp, snapshots, before):
-    kept = [] if before is None else list(before)
-    return pl.pallas_call(
-        residual_kernel,
-        grid_spec=pltpu.PrefetchScalarGridSpec(
-            num_scalar_prefetch=1,
-            grid=(4,),
-            in_specs=[
-                pl.BlockSpec((ROWS, 2 * MODES), lambda j, i: (0, 0)),
-                pl.BlockSpec((2 * MODES, PART), lambda j, i: (0, j)),
-                pl.BlockSpec((ROWS, PART), lambda j, i: (0, i[0] * 4 + j)),
-            ]
-            + [pl.BlockSpec(memory_space=pl.ANY)] * len(kept),
-            out_specs=[
-                pl.BlockSpec((ROWS, PART), lambda j, i: (0, i[0] * 4 + j)),
-                pl.BlockSpec((2 * MODES, PART), lambda j, i: (0, i[0] * 4 + j)),
-            ],
+def columns_of(quarter):
+    return pl.ds(pl.multiple_of(quarter * QUARTER, QUARTER), QUARTER)
+
+
+def fit_piece(basis_ref, amp_ref, snapshots_ref, out_ref):
+    for first in range(0, QUARTER, WIDTH):
+        here = pl.ds(first, WIDTH)
+        amp = amp_ref[:, here]
+        signed = jnp.concatenate([amp[:MODES], -amp[MODES:]], 0).astype(jnp.bfloat16)
+        fitted = jnp.dot(basis_ref[...], signed, preferred_element_type=jnp.float32)
+        out_ref[:, here] = (snapshots_ref[:, here].astype(jnp.float32) - fitted).astype(
+            jnp.bfloat16
+        )
+
+
+def own_kernel(
+    u_ref, basis_ref, amp_ref, snapshots_ref, residual_ref, amp_out_ref, rest_ref, old, new, sems
+):
+    own = columns_of(u_ref[0])
+    load = pltpu.make_async_copy(snapshots_ref.at[:, own], old, sems.at[0])
+    load.start()
+    copies = [
+        pltpu.make_async_copy(amp_ref.at[:, pl.ds(0, QUARTER)], amp_out_ref.at[:, own], sems.at[1])
+    ]
+    for n, step in enumerate(ORDER):
+        there = columns_of((u_ref[0] - step) & 3)
+        copies.append(
+            pltpu.make_async_copy(snapshots_ref.at[:, there], rest_ref.at[n], sems.at[2 + n])
+        )
+    for copy in copies:
+        copy.start()
+    load.wait()
+    fit_piece(basis_ref, amp_ref, old, new)
+    store = pltpu.make_async_copy(new, residual_ref.at[:, own], sems.at[0])
+    store.start()
+    for copy in copies:
+        copy.wait()
+    store.wait()
+
+
+def rest_kernel(u_ref, basis_ref, a1, a2, a3, rest_ref, k1, k2, residual_ref, amp_out_ref, new, sems):
+    copies = []
+    for n, (step, amp_ref) in enumerate(zip(ORDER, (a1, a2, a3))):
+        there = columns_of((u_ref[0] - step) & 3)
+        copies.append(
+            pltpu.make_async_copy(
+                amp_ref.at[:, pl.ds(0, QUARTER)], amp_out_ref.at[:, there], sems.at[n]
+            )
+        )
+        copies[-1].start()
+    for n, (step, amp_ref) in enumerate(zip(ORDER, (a1, a2, a3))):
+        there = columns_of((u_ref[0] - step) & 3)
+        fit_piece(basis_ref, amp_ref, rest_ref.at[n], new.at[n])
+        copies.append(
+            pltpu.make_async_copy(new.at[n], residual_ref.at[:, there], sems.at[3 + n])
+        )
+        copies[-1].start()
+    for copy in copies:
+        copy.wait()
+
+
+SMEM = pl.BlockSpec(memory_space=pltpu.SMEM)
+HBM = pl.BlockSpec(memory_space=pltpu.HBM)
+RESULTS = [
+    jax.ShapeDtypeStruct((ROWS, COLS), jnp.bfloat16),
+    jax.ShapeDtypeStruct((2 * MODES, COLS), jnp.float32),
+]
+
+
+def own_residual(u, basis, amp, snapshots):
+    return pl.pallas_call(
+        own_kernel,
+        in_specs=[SMEM, VMEM, VMEM, HBM],
+        out_specs=[HBM, HBM, VMEM],
+        out_shape=RESULTS + [jax.ShapeDtypeStruct((3, ROWS, QUARTER), jnp.bfloat16)],
+        scratch_shapes=[
+            pltpu.VMEM((ROWS, QUARTER), jnp.bfloat16),
+            pltpu.VMEM((ROWS, QUARTER), jnp.bfloat16),
+            pltpu.SemaphoreType.DMA((5,)),
+        ],
+        compiler_params=PARAMS,
+        cost_estimate=pl.CostEstimate(
+            flops=2 * 64 * ROWS * QUARTER, bytes_accessed=11 << 20, transcendentals=0
         ),
-        out_shape=[
-            jax.ShapeDtypeStruct((ROWS, COLS), jnp.bfloat16),
-            jax.ShapeDtypeStruct((2 * MODES, COLS), jnp.float32),
+        name="own_residual",
+    )(u, basis, amp, snapshots)
+
+
+def rest_residual(u, basis, amps, rest, residual, amp_out):
+    return pl.pallas_call(
+        rest_kernel,
+        in_specs=[SMEM, VMEM, VMEM, VMEM, VMEM, VMEM, HBM, HBM],
+        out_specs=[HBM, HBM],
+        out_shape=RESULTS,
+        input_output_aliases={6: 0, 7: 1},
+        scratch_shapes=[
+            pltpu.VMEM((3, ROWS, QUARTER), jnp.bfloat16),
+            pltpu.SemaphoreType.DMA((6,)),
         ],
-        input_output_aliases={4: 0, 5: 1} if kept else {},
         compiler_params=PARAMS,
         cost_estimate=pl.CostEstimate(
-            flops=2 * 64 * ROWS * QUARTER, bytes_accessed=5 << 20, transcendentals=0
+            flops=6 * 64 * ROWS * QUARTER, bytes_accessed=8 << 20, transcendentals=0
         ),
-        name="residual_part",
-    )(index, basis, amp, snapshots, *kept)
+        name="rest_residual",
+    )(u, basis, *amps, rest, residual, amp_out)
 
 
 def update_kernel(exponents_ref, terms_ref, here_ref, there_ref, out_ref):
@@ -300,20 +411,17 @@
 def shards(snapshots, exponents):
     z, y, x, core = place(lax.axis_index("tm") * 2 + lax.axis_index("space"))
     u = jnp.where(core == 0, x, y).astype(jnp.int32)
-    v = jnp.where(core == 0, y, x).astype(jnp.int32)
+    v = jnp.where(core == 0, y, z).astype(jnp.int32)
     at_v = v[None]
-    first_row = lax.axis_index("tm") * ROWS
-    times = (first_row + jnp.arange(ROWS, dtype=jnp.int32)).astype(jnp.float32) / TIMES
-    real, imag = waves(exponents, times)
-    basis_t = jnp.concatenate([real, imag], 0)
-    basis_t = jnp.concatenate([basis_t, times[None, :] * basis_t], 0).astype(jnp.bfloat16)
-    basis = basis_t[: 2 * MODES].T
+    basis_t, basis = make_basis(lax.axis_index("tm")[None] * ROWS, exponents)
 
     received = {}
-    for step in (2, 1, 3):
-        part = project(((u + step) & 3)[None], basis_t, snapshots)
-        received[step] = send(part, "u", step)
-    own = project(u[None], basis_t, snapshots)
+    (part,) = project(((u + 2) & 3)[None], basis_t, snapshots)
+    received[2] = send(part, "u", 2)
+    others = project(jnp.stack([(u + 1) & 3, (u + 3) & 3]), basis_t, snapshots)
+    received[1] = send(others[0], "u", 1)
+    received[3] = send(others[1], "u", 3)
+    (own,) = project(u[None], basis_t, snapshots)
 
     coarse = table(exponents, jnp.arange(COARSE, dtype=jnp.float32) / COARSE)
     fine = table(exponents, jnp.arange(FINE, dtype=jnp.float32) / TIMES)
@@ -332,22 +440,23 @@
         name="gram",
     )(coarse, fine)
 
+    own, solve, terms = lax.optimization_barrier((own, solve, terms))
     sums = first_sum(at_v, own, [received[s] for s in (1, 2, 3)])
     received = {s: send(sums[s], "v", s) for s in (2, 1, 3)}
     total = plain_sum(sums[0], [received[s] for s in (1, 2, 3)])
-    received = {s: send(total, "z", s) for s in (2, 1, 3)}
+    received = {s: send(total, "w", s) for s in (2, 1, 3)}
     amp = amplitudes_of(solve, total, [received[s] for s in (1, 2, 3)])
     received = {s: send(amp, "v", s) for s in (2, 1, 3)}
     amp = join(at_v, amp, [received[s] for s in (1, 2, 3)])
     received = {s: send(amp, "u", s) for s in (2, 1, 3)}
-    out = residual_part(u[None], basis, amp, snapshots, None)
+    residual, amp_out, rest = own_residual(u[None], basis, amp, snapshots)
     sums = plain_sum(
         amp[:, QUARTER:], [received[s][:, QUARTER:] for s in (1, 2, 3)]
     )
     other = swap_cores(sums)
-    for step in (1, 3, 2):
-        out = residual_part(((u - step) & 3)[None], basis, received[step], snapshots, out)
-    residual, amp = out
+    residual, amp_out = rest_residual(
+        u[None], basis, [received[step] for step in ORDER], rest, residual, amp_out
+    )
     new_exponents = pl.pallas_call(
         update_kernel,
         in_specs=[VMEM] * 4,
@@ -356,7 +465,7 @@
         compiler_params=PARAMS,
         name="update",
     )(exponents, terms, sums, other)
-    return (new_exponents, amp.reshape(2, MODES, COLS), residual)
+    return (new_exponents, amp_out.reshape(2, MODES, COLS), residual)
 
 
 def solution(mesh):

time: 118 us -> 99.6 us (0.84)
  Pallas kernels: 40.7 us -> 26.2 us
  waiting for transfers between devices: 46.7 us -> 42 us
  starting transfers between devices: 26.5 us -> 27.7 us
    pallas_call x4 -> x3, Pallas kernels: 17.3 us -> 7.7 us  [the longest x1 3.84 us: own_residual(): pl.pallas_call(own_kernel, in_specs=[SMEM, VMEM, VMEM, HBM], out_specs=[H...]
    pallas_call x4 -> x3, Pallas kernels: 13.7 us -> 8.79 us  [project(): pl.pallas_call(project_kernel, grid_spec=pltpu.PrefetchScalarGridSpec(num...]
    ppermute x15, waiting for transfers between devices: 46.7 us -> 42 us  [send(): return lax.ppermute(value, ('tm', 'space'), shifted(axis, step))]
    ppermute x1, starting transfers between devices: 4.1 us -> 5.81 us  [swap_cores(): lax.ppermute(value, ('tm', 'space'), [(d, d ^ 1) for d in range(128)])]
    mul x2, other arithmetic: 0.33 us -> 1.6 us  [waves(): return (magnitude * jnp.cos(phase_angle), magnitude * jnp.sin(phase_angle))]
  transfers between devices with their start and end apart: 16 -> 16, of which waited for: 12 -> 12; matrix products, arithmetic and copies ran while one was open for 0% -> 2% of each run, Pallas kernels for 27% -> 18%
where the time goes in v2:
time: 99.6 us; the launch traced here: 99.4 us
  waiting for transfers between devices  42 us (42%)
  starting transfers between devices  27.7 us (28%)
  Pallas kernels  26.2 us (26%)
  other arithmetic  1.78 us (2%)
    ppermute x15, waiting for transfers between devices, send(): return lax.ppermute(value, ('tm', 'space'), shifted(axis, step))  42 us
    ppermute x15, starting transfers between devices, send(): return lax.ppermute(value, ('tm', 'space'), shifted(axis, step))  21.9 us
    pallas_call x3, Pallas kernels, project(): pl.pallas_call(project_kernel, grid_spec=pltpu.PrefetchScalarGridSpec(num...  8.79 us
    ppermute x1, starting transfers between devices, swap_cores(): lax.ppermute(value, ('tm', 'space'), [(d, d ^ 1) for d in range(128)])  5.81 us
    pallas_call x1, Pallas kernels, shards(): pl.pallas_call(gram_kernel, in_specs=[VMEM] * 2, out_specs=[VMEM] * 2, ou...  3.85 us
    pallas_call x1, Pallas kernels, own_residual(): pl.pallas_call(own_kernel, in_specs=[SMEM, VMEM, VMEM, HBM], out_specs=[H...  3.84 us
    pallas_call x1, Pallas kernels, shards(): pl.pallas_call(update_kernel, in_specs=[VMEM] * 4, out_specs=VMEM, out_sh...  3.73 us
    pallas_call x1, Pallas kernels, rest_residual(): pl.pallas_call(rest_kernel, in_specs=[SMEM, VMEM, VMEM, VMEM, VMEM, VMEM,...  3.44 us
  transfers between devices with their start and end apart: 16, of which 12 were waited for; matrix products, arithmetic and copies ran while one was open for 2% of the time, Pallas kernels for 18%

profile of v2, /device:TPU:1, one launch (start us, length us, event | category | flops | bytes accessed | tf_op | source)
XLA Modules:
  0.0 99.4 jit_solution(17689102751119234787)
XLA Ops:
  0.7 0.7 copy-done
  1.8 2.0 %project.5 = f32[4,128,512]{2,1,0:T(8,128)S(1)} custom-call(s32[1]{0:T(128)} %bitcast.17.index_ref, bf16[128,512]{1,0:T(8,128)(2,1)S(1)} %get-tuple-element.21.basis_ref, bf16[512,8192]{1,0:T(8,128)(2,1)} %snapshots_ref.7), custom_call_target="tpu_custom_call" | custom-call | flops 268435456 | bytes 3145728 | tf_op jit(solution)/shard_map/project/pallas_call | solution.py:183
  3.8 3.8 %collective-permute-start.1 = (f32[4,128,512]{2,1,0:T(8,128)S(1)}, f32[4,128,512]{2,1,0:T(8,128)S(1)}, u32[]{:S(2)}, u32[]{:S(2)}) collective-permute-start(f32[4,128,512]{2,1,0:T(8,128)S(1)} %project.5), channel_id=1, source_target_pairs={{0,4},{1,17},{2,6},{3,19},{4,0},{5,21},{6,2},{7,23},{8,12},{9,25},... | collective-permute-start | bytes 3145736 | tf_op jit(solution)/shard_map/ppermute | solution.py:46
  7.7 4.6 %project.4 = (f32[4,128,512]{2,1,0:T(8,128)}, f32[4,128,512]{2,1,0:T(8,128)}) custom-call(s32[2]{0:T(128)S(1)} %pad_add_fusion.index_ref, bf16[128,512]{1,0:T(8,128)(2,1)S(1)} %get-tuple-element.21.basis_ref, bf16[512,8192]{1,0:T(8,128)(2,1)} %snapshots_ref.7), custom_call_target="tpu_custom_call" | custom-call | flops 536870912 | bytes 6291456 | tf_op jit(solution)/shard_map/project/pallas_call | solution.py:183
  12.7 2.3 %collective-permute-start.2 = (f32[4,128,512]{2,1,0:T(8,128)}, f32[4,128,512]{2,1,0:T(8,128)}, u32[]{:S(2)}, u32[]{:S(2)}) collective-permute-start(f32[4,128,512]{2,1,0:T(8,128)} %get-tuple-element.28), channel_id=1, source_target_pairs={{0,6},{1,25},{2,0},{3,27},{4,2},{5,29},{6,4},{7,31},{8,14},{9,1},{... | collective-permute-start | bytes 3145736 | tf_op jit(solution)/shard_map/ppermute | solution.py:46
  15.0 0.8 fusion
  15.8 0.8 fusion.2
  16.7 2.2 %project.3.own_ref = f32[4,128,512]{2,1,0:T(8,128)S(1)} custom-call(s32[1]{0:T(128)} %bitcast.index_ref.u_ref, bf16[128,512]{1,0:T(8,128)(2,1)S(1)} %get-tuple-element.21.basis_ref, bf16[512,8192]{1,0:T(8,128)(2,1)} %snapshots_ref.7), custom_call_target="tpu_custom_call" | custom-call | flops 268435456 | bytes 3145728 | tf_op jit(solution)/shard_map/project/pallas_call | solution.py:183
  19.1 3.9 %gram.1 = (f32[64,64]{1,0:T(8,128)S(1)}, f32[4,32,32]{2,1,0:T(8,128)S(1)}) custom-call(f32[4,32,512]{2,1,0:T(8,128)S(1)} %pad_maximum_fusion.coarse_ref, f32[4,32,256]{2,1,0:T(8,128)S(1)} %pad_maximum_fusion.1.fine_ref), custom_call_target="tpu_custom_call" | custom-call | flops 1073741824 | bytes 16777216 | tf_op jit(solution)/shard_map/gram/pallas_call | solution.py:428
  23.0 8.4 %collective-permute-done.r1_ref = f32[4,128,512]{2,1,0:T(8,128)S(1)} collective-permute-done((f32[4,128,512]{2,1,0:T(8,128)}, f32[4,128,512]{2,1,0:T(8,128)S(1)}, u32[]{:S(2)}, u32[]{:S(2)}) %collective-permute-start) | collective-permute-done | bytes 1048608 | tf_op jit(solution)/shard_map/ppermute | solution.py:46
  31.9 1.4 %first_sum.1 = (f32[128,512]{1,0:T(8,128)S(1)}, f32[128,512]{1,0:T(8,128)S(1)}, f32[128,512]{1,0:T(8,128)S(1)}, f32[128,512]{1,0:T(8,128)S(1)}) custom-call(s32[1]{0:T(128)} %bitcast.14.v_ref, f32[4,128,512]{2,1,0:T(8,128)S(1)} %project.3.own_ref, f32[4,128,512]{2,1,0:T(8,128)S(1)} %collective-permute-done.r1_ref, ...), custom_call_target="tpu_custom_call" | custom-call | tf_op jit(solution)/shard_map/first_sum/pallas_call | solution.py:212
  33.3 1.7 %collective-permute-start.3 = (f32[128,512]{1,0:T(8,128)S(1)}, f32[128,512]{1,0:T(8,128)S(1)}, u32[]{:S(2)}, u32[]{:S(2)}) collective-permute-start(f32[128,512]{1,0:T(8,128)S(1)} %get-tuple-element.30), channel_id=1, source_target_pairs={{0,8},{1,33},{2,10},{3,35},{4,12},{5,37},{6,14},{7,39},{8,16},{9,4... | collective-permute-start | bytes 786440 | tf_op jit(solution)/shard_map/ppermute | solution.py:46
  35.0 3.3 %collective-permute-start.4 = (f32[128,512]{1,0:T(8,128)S(1)}, f32[128,512]{1,0:T(8,128)S(1)}, u32[]{:S(2)}, u32[]{:S(2)}) collective-permute-start(f32[128,512]{1,0:T(8,128)S(1)} %get-tuple-element.31), channel_id=1, source_target_pairs={{0,16},{1,65},{2,18},{3,67},{4,20},{5,69},{6,22},{7,71},{8,24},{9,... | collective-permute-start | bytes 786440 | tf_op jit(solution)/shard_map/ppermute | solution.py:46
  38.3 0.7 collective-permute-start.5
  39.1 2.1 %collective-permute-done.3.r1_ref = f32[128,512]{1,0:T(8,128)S(1)} collective-permute-done((f32[128,512]{1,0:T(8,128)S(1)}, f32[128,512]{1,0:T(8,128)S(1)}, u32[]{:S(2)}, u32[]{:S(2)}) %collective-permute-start.3) | collective-permute-done | bytes 262176 | tf_op jit(solution)/shard_map/ppermute | solution.py:46
  41.2 4.0 %collective-permute-done.4.r2_ref = f32[128,512]{1,0:T(8,128)S(1)} collective-permute-done((f32[128,512]{1,0:T(8,128)S(1)}, f32[128,512]{1,0:T(8,128)S(1)}, u32[]{:S(2)}, u32[]{:S(2)}) %collective-permute-start.4) | collective-permute-done | bytes 262176 | tf_op jit(solution)/shard_map/ppermute | solution.py:46
  45.3 2.5 %collective-permute-start.8 = (f32[128,512]{1,0:T(8,128)S(1)}, f32[128,512]{1,0:T(8,128)S(1)}, u32[]{:S(2)}, u32[]{:S(2)}) collective-permute-start(f32[128,512]{1,0:T(8,128)S(1)} %plain_sum.2.own_ref), channel_id=1, source_target_pairs={{0,96},{1,7},{2,98},{3,1},{4,100},{5,3},{6,102},{7,5},{8,104},{9,1... | collective-permute-start | bytes 786440 | tf_op jit(solution)/shard_map/ppermute | solution.py:46
  48.8 5.1 %collective-permute-done.8.r3_ref = f32[128,512]{1,0:T(8,128)S(1)} collective-permute-done((f32[128,512]{1,0:T(8,128)S(1)}, f32[128,512]{1,0:T(8,128)S(1)}, u32[]{:S(2)}, u32[]{:S(2)}) %collective-permute-start.8) | collective-permute-done | bytes 262176 | tf_op jit(solution)/shard_map/ppermute | solution.py:46
  53.9 0.7 collective-permute-done.7.r2_ref
  54.6 3.0 %collective-permute-done.6.r1_ref = f32[128,512]{1,0:T(8,128)S(1)} collective-permute-done((f32[128,512]{1,0:T(8,128)S(1)}, f32[128,512]{1,0:T(8,128)S(1)}, u32[]{:S(2)}, u32[]{:S(2)}) %collective-permute-start.6) | collective-permute-done | bytes 262176 | tf_op jit(solution)/shard_map/ppermute | solution.py:46
  58.2 1.9 %collective-permute-start.11 = (f32[64,640]{1,0:T(8,128)S(1)}, f32[64,640]{1,0:T(8,128)S(1)}, u32[]{:S(2)}, u32[]{:S(2)}) collective-permute-start(f32[64,640]{1,0:T(8,128)S(1)} %amplitudes.1.own_ref), channel_id=1, source_target_pairs={{0,24},{1,97},{2,26},{3,99},{4,28},{5,101},{6,30},{7,103},{8,0},{9... | collective-permute-start | bytes 491528 | tf_op jit(solution)/shard_map/ppermute | solution.py:46
  60.2 0.6 collective-permute-start.10
  60.8 3.3 %collective-permute-done.11.r3_ref = f32[64,640]{1,0:T(8,128)S(1)} collective-permute-done((f32[64,640]{1,0:T(8,128)S(1)}, f32[64,640]{1,0:T(8,128)S(1)}, u32[]{:S(2)}, u32[]{:S(2)}) %collective-permute-start.11) | collective-permute-done | bytes 163872 | tf_op jit(solution)/shard_map/ppermute | solution.py:46
  64.2 1.8 %collective-permute-done.10.r2_ref = f32[64,640]{1,0:T(8,128)S(1)} collective-permute-done((f32[64,640]{1,0:T(8,128)S(1)}, f32[64,640]{1,0:T(8,128)S(1)}, u32[]{:S(2)}, u32[]{:S(2)}) %collective-permute-start.10) | collective-permute-done | bytes 163872 | tf_op jit(solution)/shard_map/ppermute | solution.py:46
  65.9 1.7 %collective-permute-done.9.r1_ref = f32[64,640]{1,0:T(8,128)S(1)} collective-permute-done((f32[64,640]{1,0:T(8,128)S(1)}, f32[64,640]{1,0:T(8,128)S(1)}, u32[]{:S(2)}, u32[]{:S(2)}) %collective-permute-start.9) | collective-permute-done | bytes 163872 | tf_op jit(solution)/shard_map/ppermute | solution.py:46
  67.6 2.6 %collective-permute-start.14 = (f32[64,2176]{1,0:T(8,128)S(1)}, f32[64,2176]{1,0:T(8,128)S(1)}, u32[]{:S(2)}, u32[]{:S(2)}) collective-permute-start(f32[64,2176]{1,0:T(8,128)S(1)} %join.1.amp_ref), channel_id=1, source_target_pairs={{0,6},{1,25},{2,0},{3,27},{4,2},{5,29},{6,4},{7,31},{8,14},{9,1},{... | collective-permute-start | bytes 1671176 | tf_op jit(solution)/shard_map/ppermute | solution.py:46
  71.1 3.8 %own_residual.1 = (bf16[512,8192]{1,0:T(8,128)(2,1)}, f32[64,8192]{1,0:T(8,128)}, bf16[3,512,2048]{2,1,0:T(8,128)(2,1)S(1)}) custom-call(s32[1]{0:T(128)} %bitcast.index_ref.u_ref, bf16[512,64]{1,0:T(8,128)(2,1)S(1)} %get-tuple-element.33.basis_ref, f32[64,2176]{1,0:T(8,128)S(1)} %join.1.amp_ref, bf16[512,8192]{1,0:T(8,128)(2,1)S(1)} %bitcast.32), custom_call_target="tpu_custom_call" | custom-call | flops 134217728 | bytes 11534336 | tf_op jit(solution)/shard_map/own_residual/pallas_call | solution.py:351
  75.0 7.8 %collective-permute-done.14.a2 = f32[64,2176]{1,0:T(8,128)S(1)} collective-permute-done((f32[64,2176]{1,0:T(8,128)S(1)}, f32[64,2176]{1,0:T(8,128)S(1)}, u32[]{:S(2)}, u32[]{:S(2)}) %collective-permute-start.14) | collective-permute-done | bytes 557088 | tf_op jit(solution)/shard_map/ppermute | solution.py:46
  82.7 3.7 %collective-permute-done.12.a1 = f32[64,2176]{1,0:T(8,128)S(1)} collective-permute-done((f32[64,2176]{1,0:T(8,128)S(1)}, f32[64,2176]{1,0:T(8,128)S(1)}, u32[]{:S(2)}, u32[]{:S(2)}) %collective-permute-start.12) | collective-permute-done | bytes 557088 | tf_op jit(solution)/shard_map/ppermute | solution.py:46
  86.4 5.8 %collective-permute-start.15 = (f32[64,128]{1,0:T(8,128)S(1)}, f32[64,128]{1,0:T(8,128)S(1)}, u32[]{:S(2)}, u32[]{:S(2)}) collective-permute-start(f32[64,128]{1,0:T(8,128)S(1)} %plain_sum.3.here_ref), channel_id=1, source_target_pairs={{0,1},{1,0},{2,3},{3,2},{4,5},{5,4},{6,7},{7,6},{8,9},{9,8},{10,11... | collective-permute-start | bytes 98312 | tf_op jit(solution)/shard_map/ppermute | solution.py:50
  92.2 3.4 %rest_residual.1 = (bf16[512,8192]{1,0:T(8,128)(2,1)}, f32[64,8192]{1,0:T(8,128)}) custom-call(s32[1]{0:T(128)} %bitcast.index_ref.u_ref, bf16[512,64]{1,0:T(8,128)(2,1)S(1)} %get-tuple-element.33.basis_ref, f32[64,2176]{1,0:T(8,128)S(1)} %collective-permute-done.12.a1, ...), custom_call_target="tpu_custom_call", output_to_operand_aliasing={{0}: (6, {}), {1}: (7, {})} | custom-call | flops 402653184 | bytes 8388608 | tf_op jit(solution)/shard_map/rest_residual/pallas_call | solution.py:370
  95.7 3.7 %update.1 = f32[2,32]{1,0:T(2,128)} custom-call(f32[2,32]{1,0:T(2,128)S(1)} %copy-done.1, f32[4,32,32]{2,1,0:T(8,128)S(1)} %get-tuple-element.24.terms_ref, f32[64,128]{1,0:T(8,128)S(1)} %plain_sum.3.here_ref, f32[64,128]{1,0:T(8,128)S(1)} %collective-permute-done.15.there_ref), custom_call_target="tpu_custom_call" | custom-call | tf_op jit(solution)/shard_map/update/pallas_call | solution.py:460
  (56 shorter events, 4.2 us)
Async XLA Ops:
  0.6 0.7 copy-start
  1.8 13.2 %copy-start.1 = (f32[2,32]{1,0:T(2,128)S(1)}, f32[2,32]{1,0:T(2,128)}, u32[]{:S(2)}) copy-start(f32[2,32]{1,0:T(2,128)} %exponents_ref.3) | copy-start | bytes 772
  3.8 19.2 %collective-permute-start.1 = (f32[4,128,512]{2,1,0:T(8,128)S(1)}, f32[4,128,512]{2,1,0:T(8,128)S(1)}, u32[]{:S(2)}, u32[]{:S(2)}) collective-permute-start(f32[4,128,512]{2,1,0:T(8,128)S(1)} %project.5), channel_id=1, source_target_pairs={{0,4},{1,17},{2,6},{3,19},{4,0},{5,21},{6,2},{7,23},{8,12},{9,25},... | collective-permute-start | bytes 3145736 | tf_op jit(solution)/shard_map/ppermute | solution.py:46
  12.3 19.1 %collective-permute-start = (f32[4,128,512]{2,1,0:T(8,128)}, f32[4,128,512]{2,1,0:T(8,128)S(1)}, u32[]{:S(2)}, u32[]{:S(2)}) collective-permute-start(f32[4,128,512]{2,1,0:T(8,128)} %get-tuple-element.27), channel_id=1, source_target_pairs={{0,2},{1,9},{2,4},{3,11},{4,6},{5,13},{6,0},{7,15},{8,10},{9,17},{... | collective-permute-start | bytes 3145736 | tf_op jit(solution)/shard_map/ppermute | solution.py:46
  12.7 19.2 %collective-permute-start.2 = (f32[4,128,512]{2,1,0:T(8,128)}, f32[4,128,512]{2,1,0:T(8,128)}, u32[]{:S(2)}, u32[]{:S(2)}) collective-permute-start(f32[4,128,512]{2,1,0:T(8,128)} %get-tuple-element.28), channel_id=1, source_target_pairs={{0,6},{1,25},{2,0},{3,27},{4,2},{5,29},{6,4},{7,31},{8,14},{9,1},{... | collective-permute-start | bytes 3145736 | tf_op jit(solution)/shard_map/ppermute | solution.py:46
  16.6 2.3 %copy-start.7 = (f32[32,128]{1,0:T(8,128)S(1)}, f32[32,128]{1,0:T(8,128)}, u32[]{:S(2)}) copy-start(f32[32,128]{1,0:T(8,128)} %get-tuple-element.53) | copy-start | bytes 49156
  16.6 2.3 %copy-start.8 = (f32[32,128]{1,0:T(8,128)S(1)}, f32[32,128]{1,0:T(8,128)}, u32[]{:S(2)}) copy-start(f32[32,128]{1,0:T(8,128)} %get-tuple-element.56) | copy-start | bytes 49156
  16.6 2.3 %copy-start.9 = (f32[32,128]{1,0:T(8,128)S(1)}, f32[32,128]{1,0:T(8,128)}, u32[]{:S(2)}) copy-start(f32[32,128]{1,0:T(8,128)} %get-tuple-element.58) | copy-start | bytes 49156
  16.6 2.3 %copy-start.2 = (f32[32,256]{1,0:T(8,128)S(1)}, f32[32,256]{1,0:T(8,128)}, u32[]{:S(2)}) copy-start(f32[32,256]{1,0:T(8,128)} %get-tuple-element.50) | copy-start | bytes 98308
  16.7 2.3 %copy-start.3 = (f32[32,256]{1,0:T(8,128)S(1)}, f32[32,256]{1,0:T(8,128)}, u32[]{:S(2)}) copy-start(f32[32,256]{1,0:T(8,128)} %get-tuple-element.52) | copy-start | bytes 98308
  16.7 2.3 %copy-start.4 = (f32[1,32,128]{2,1,0:T(8,128)S(1)}, f32[1,32,128]{2,1,0:T(8,128)}, u32[]{:S(2)}) copy-start(f32[1,32,128]{2,1,0:T(8,128)} %get-tuple-element.54) | copy-start | bytes 49156
  16.7 2.3 %copy-start.5 = (f32[1,32,128]{2,1,0:T(8,128)S(1)}, f32[1,32,128]{2,1,0:T(8,128)}, u32[]{:S(2)}) copy-start(f32[1,32,128]{2,1,0:T(8,128)} %get-tuple-element.55) | copy-start | bytes 49156
  16.7 2.3 %copy-start.6 = (f32[1,32,128]{2,1,0:T(8,128)S(1)}, f32[1,32,128]{2,1,0:T(8,128)}, u32[]{:S(2)}) copy-start(f32[1,32,128]{2,1,0:T(8,128)} %get-tuple-element.57) | copy-start | bytes 49156
  16.7 54.4 %slice-start = ((s8[8388608]{0:T(1024)(128)(4,1)}), s8[4194304]{0:T(1024)(128)(4,1)S(1)}, s32[]{:S(2)}) async-start(s8[8388608]{0:T(1024)(128)(4,1)} %bitcast.31), calls=%async_computation | async-start | bytes 8388608
  19.1 52.0 %slice-start.1 = ((s8[8388608]{0:T(1024)(128)(4,1)}), s8[4194304]{0:T(1024)(128)(4,1)S(1)}, s32[]{:S(2)}) async-start(s8[8388608]{0:T(1024)(128)(4,1)} %bitcast.31), calls=%async_computation.1 | async-start | bytes 8388608
  33.3 7.9 %collective-permute-start.3 = (f32[128,512]{1,0:T(8,128)S(1)}, f32[128,512]{1,0:T(8,128)S(1)}, u32[]{:S(2)}, u32[]{:S(2)}) collective-permute-start(f32[128,512]{1,0:T(8,128)S(1)} %get-tuple-element.30), channel_id=1, source_target_pairs={{0,8},{1,33},{2,10},{3,35},{4,12},{5,37},{6,14},{7,39},{8,16},{9,4... | collective-permute-start | bytes 786440 | tf_op jit(solution)/shard_map/ppermute | solution.py:46
  35.0 10.2 %collective-permute-start.4 = (f32[128,512]{1,0:T(8,128)S(1)}, f32[128,512]{1,0:T(8,128)S(1)}, u32[]{:S(2)}, u32[]{:S(2)}) collective-permute-start(f32[128,512]{1,0:T(8,128)S(1)} %get-tuple-element.31), channel_id=1, source_target_pairs={{0,16},{1,65},{2,18},{3,67},{4,20},{5,69},{6,22},{7,71},{8,24},{9,... | collective-permute-start | bytes 786440 | tf_op jit(solution)/shard_map/ppermute | solution.py:46
  38.3 6.9 %collective-permute-start.5 = (f32[128,512]{1,0:T(8,128)S(1)}, f32[128,512]{1,0:T(8,128)S(1)}, u32[]{:S(2)}, u32[]{:S(2)}) collective-permute-start(f32[128,512]{1,0:T(8,128)S(1)} %get-tuple-element.32), channel_id=1, source_target_pairs={{0,24},{1,97},{2,26},{3,99},{4,28},{5,101},{6,30},{7,103},{8,0},{9... | collective-permute-start | bytes 786440 | tf_op jit(solution)/shard_map/ppermute | solution.py:46
  45.3 8.7 %collective-permute-start.8 = (f32[128,512]{1,0:T(8,128)S(1)}, f32[128,512]{1,0:T(8,128)S(1)}, u32[]{:S(2)}, u32[]{:S(2)}) collective-permute-start(f32[128,512]{1,0:T(8,128)S(1)} %plain_sum.2.own_ref), channel_id=1, source_target_pairs={{0,96},{1,7},{2,98},{3,1},{4,100},{5,3},{6,102},{7,5},{8,104},{9,1... | collective-permute-start | bytes 786440 | tf_op jit(solution)/shard_map/ppermute | solution.py:46
  47.8 6.8 %collective-permute-start.7 = (f32[128,512]{1,0:T(8,128)S(1)}, f32[128,512]{1,0:T(8,128)S(1)}, u32[]{:S(2)}, u32[]{:S(2)}) collective-permute-start(f32[128,512]{1,0:T(8,128)S(1)} %plain_sum.2.own_ref), channel_id=1, source_target_pairs={{0,64},{1,5},{2,66},{3,7},{4,68},{5,1},{6,70},{7,3},{8,72},{9,13},... | collective-permute-start | bytes 786440 | tf_op jit(solution)/shard_map/ppermute | solution.py:46
  48.3 9.3 %collective-permute-start.6 = (f32[128,512]{1,0:T(8,128)S(1)}, f32[128,512]{1,0:T(8,128)S(1)}, u32[]{:S(2)}, u32[]{:S(2)}) collective-permute-start(f32[128,512]{1,0:T(8,128)S(1)} %plain_sum.2.own_ref), channel_id=1, source_target_pairs={{0,32},{1,3},{2,34},{3,5},{4,36},{5,7},{6,38},{7,1},{8,40},{9,11},... | collective-permute-start | bytes 786440 | tf_op jit(solution)/shard_map/ppermute | solution.py:46
  58.2 6.0 %collective-permute-start.11 = (f32[64,640]{1,0:T(8,128)S(1)}, f32[64,640]{1,0:T(8,128)S(1)}, u32[]{:S(2)}, u32[]{:S(2)}) collective-permute-start(f32[64,640]{1,0:T(8,128)S(1)} %amplitudes.1.own_ref), channel_id=1, source_target_pairs={{0,24},{1,97},{2,26},{3,99},{4,28},{5,101},{6,30},{7,103},{8,0},{9... | collective-permute-start | bytes 491528 | tf_op jit(solution)/shard_map/ppermute | solution.py:46
  60.2 5.8 %collective-permute-start.10 = (f32[64,640]{1,0:T(8,128)S(1)}, f32[64,640]{1,0:T(8,128)S(1)}, u32[]{:S(2)}, u32[]{:S(2)}) collective-permute-start(f32[64,640]{1,0:T(8,128)S(1)} %amplitudes.1.own_ref), channel_id=1, source_target_pairs={{0,16},{1,65},{2,18},{3,67},{4,20},{5,69},{6,22},{7,71},{8,24},{9,... | collective-permute-start | bytes 491528 | tf_op jit(solution)/shard_map/ppermute | solution.py:46
  60.7 6.9 %collective-permute-start.9 = (f32[64,640]{1,0:T(8,128)S(1)}, f32[64,640]{1,0:T(8,128)S(1)}, u32[]{:S(2)}, u32[]{:S(2)}) collective-permute-start(f32[64,640]{1,0:T(8,128)S(1)} %amplitudes.1.own_ref), channel_id=1, source_target_pairs={{0,8},{1,33},{2,10},{3,35},{4,12},{5,37},{6,14},{7,39},{8,16},{9,4... | collective-permute-start | bytes 491528 | tf_op jit(solution)/shard_map/ppermute | solution.py:46
  67.6 15.1 %collective-permute-start.14 = (f32[64,2176]{1,0:T(8,128)S(1)}, f32[64,2176]{1,0:T(8,128)S(1)}, u32[]{:S(2)}, u32[]{:S(2)}) collective-permute-start(f32[64,2176]{1,0:T(8,128)S(1)} %join.1.amp_ref), channel_id=1, source_target_pairs={{0,6},{1,25},{2,0},{3,27},{4,2},{5,29},{6,4},{7,31},{8,14},{9,1},{... | collective-permute-start | bytes 1671176 | tf_op jit(solution)/shard_map/ppermute | solution.py:46
  70.3 12.5 %collective-permute-start.13 = (f32[64,2176]{1,0:T(8,128)S(1)}, f32[64,2176]{1,0:T(8,128)S(1)}, u32[]{:S(2)}, u32[]{:S(2)}) collective-permute-start(f32[64,2176]{1,0:T(8,128)S(1)} %join.1.amp_ref), channel_id=1, source_target_pairs={{0,4},{1,17},{2,6},{3,19},{4,0},{5,21},{6,2},{7,23},{8,12},{9,25},... | collective-permute-start | bytes 1671176 | tf_op jit(solution)/shard_map/ppermute | solution.py:46
  70.5 15.9 %collective-permute-start.12 = (f32[64,2176]{1,0:T(8,128)S(1)}, f32[64,2176]{1,0:T(8,128)S(1)}, u32[]{:S(2)}, u32[]{:S(2)}) collective-permute-start(f32[64,2176]{1,0:T(8,128)S(1)} %join.1.amp_ref), channel_id=1, source_target_pairs={{0,2},{1,9},{2,4},{3,11},{4,6},{5,13},{6,0},{7,15},{8,10},{9,17},{... | collective-permute-start | bytes 1671176 | tf_op jit(solution)/shard_map/ppermute | solution.py:46
  86.4 9.3 %collective-permute-start.15 = (f32[64,128]{1,0:T(8,128)S(1)}, f32[64,128]{1,0:T(8,128)S(1)}, u32[]{:S(2)}, u32[]{:S(2)}) collective-permute-start(f32[64,128]{1,0:T(8,128)S(1)} %plain_sum.3.here_ref), channel_id=1, source_target_pairs={{0,1},{1,0},{2,3},{3,2},{4,5},{5,4},{6,7},{7,6},{8,9},{9,8},{10,11... | collective-permute-start | bytes 98312 | tf_op jit(solution)/shard_map/ppermute | solution.py:50

commit v3 on v2

--- a/solution.py
+++ b/solution.py
@@ -20,7 +20,7 @@
 VMEM = pl.BlockSpec(memory_space=pltpu.VMEM)
 PARAMS = pltpu.CompilerParams(vmem_limit_bytes=24 * 1024 * 1024)
 WIDE_PARAMS = pltpu.CompilerParams(vmem_limit_bytes=52 * 1024 * 1024)
-AXES = {"u": "xy", "v": "yz", "w": "zx"}
+AXES = {"u": "xz", "v": "yx", "w": "zy"}
 
 
 def place(device):
@@ -167,7 +167,7 @@
 
 
 def project_kernel(index_ref, basis_ref, snapshots_ref, *out_refs):
-    for step, out_ref in enumerate(out_refs):
+    for step in range(len(out_refs) // 2):
 
         @pl.when(pl.program_id(0) == step)
         def _():
@@ -175,7 +175,7 @@
                 basis_ref[...], snapshots_ref[...], preferred_element_type=jnp.float32
             )
             for j in range(4):
-                out_ref[j] = found[:, j * PART : (j + 1) * PART]
+                out_refs[2 * step + j // 2][j % 2] = found[:, j * PART : (j + 1) * PART]
 
 
 def project(indices, basis_t, snapshots):
@@ -189,9 +189,9 @@
                 pl.BlockSpec((4 * MODES, ROWS), lambda j, i: (0, 0)),
                 pl.BlockSpec((ROWS, QUARTER), lambda j, i: (0, i[j])),
             ],
-            out_specs=[pl.BlockSpec((4, 4 * MODES, PART), lambda j, i: (0, 0, 0))] * count,
+            out_specs=[pl.BlockSpec((2, 4 * MODES, PART), lambda j, i: (0, 0, 0))] * (2 * count),
         ),
-        out_shape=[jax.ShapeDtypeStruct((4, 4 * MODES, PART), jnp.float32)] * count,
+        out_shape=[jax.ShapeDtypeStruct((2, 4 * MODES, PART), jnp.float32)] * (2 * count),
         compiler_params=WIDE_PARAMS,
         cost_estimate=pl.CostEstimate(
             flops=count * 2 * 128 * ROWS * QUARTER,
@@ -202,21 +202,43 @@
     )(indices, basis_t, snapshots)
 
 
-def first_sum_kernel(v_ref, own_ref, r1_ref, r2_ref, r3_ref, *out_refs):
+def relay_kernel(low_ref, high_ref, from_left_ref, from_right_ref, low_out_ref, high_out_ref):
+    low_out_ref[...] = low_ref[...] + from_left_ref[...]
+    high_out_ref[...] = high_ref[...] + from_right_ref[...]
+
+
+def relay(low, high, from_left, from_right):
+    return pl.pallas_call(
+        relay_kernel,
+        in_specs=[VMEM] * 4,
+        out_specs=[VMEM] * 2,
+        out_shape=[jax.ShapeDtypeStruct((2, 4 * MODES, PART), jnp.float32)] * 2,
+        compiler_params=PARAMS,
+        name="relay",
+    )(low, high, from_left, from_right)
+
+
+def first_sum_kernel(v_ref, *refs):
+    out_refs = refs[6:]
     for step in range(4):
         j = (v_ref[0] + step) & 3
-        out_refs[step][...] = (own_ref[j] + r2_ref[j]) + (r1_ref[j] + r3_ref[j])
-
-
-def first_sum(v, own, received):
+        for half in range(2):
+
+            @pl.when((j >> 1) == half)
+            def _():
+                a, b, c = (ref[j & 1] for ref in refs[3 * half : 3 * half + 3])
+                out_refs[step][...] = (a + b) + c
+
+
+def first_sum(v, low, high):
     return pl.pallas_call(
         first_sum_kernel,
-        in_specs=[pl.BlockSpec(memory_space=pltpu.SMEM)] + [VMEM] * 4,
+        in_specs=[pl.BlockSpec(memory_space=pltpu.SMEM)] + [VMEM] * 6,
         out_specs=[VMEM] * 4,
         out_shape=[jax.ShapeDtypeStruct((4 * MODES, PART), jnp.float32)] * 4,
         compiler_params=PARAMS,
         name="first_sum",
-    )(v, own, *received)
+    )(v, *low, *high)
 
 
 def sum_kernel(own_ref, r1_ref, r2_ref, r3_ref, out_ref):
@@ -410,18 +432,24 @@
 
 def shards(snapshots, exponents):
     z, y, x, core = place(lax.axis_index("tm") * 2 + lax.axis_index("space"))
-    u = jnp.where(core == 0, x, y).astype(jnp.int32)
-    v = jnp.where(core == 0, y, z).astype(jnp.int32)
+    u = jnp.where(core == 0, x, z).astype(jnp.int32)
+    v = jnp.where(core == 0, y, x).astype(jnp.int32)
     at_v = v[None]
     basis_t, basis = make_basis(lax.axis_index("tm")[None] * ROWS, exponents)
 
-    received = {}
-    (part,) = project(((u + 2) & 3)[None], basis_t, snapshots)
-    received[2] = send(part, "u", 2)
-    others = project(jnp.stack([(u + 1) & 3, (u + 3) & 3]), basis_t, snapshots)
-    received[1] = send(others[0], "u", 1)
-    received[3] = send(others[1], "u", 3)
-    (own,) = project(u[None], basis_t, snapshots)
+    low, high = project(((u + 2) & 3)[None], basis_t, snapshots)
+    from_left = send(low, "u", 1)
+    from_right = send(high, "u", 3)
+    right_low, right_high, left_low, left_high = project(
+        jnp.stack([(u + 1) & 3, (u + 3) & 3]), basis_t, snapshots
+    )
+    direct_high = send(right_high, "u", 1)
+    direct_low = send(left_low, "u", 3)
+    right_low, left_high = relay(right_low, left_high, from_left, from_right)
+    relayed_low = send(right_low, "u", 1)
+    relayed_high = send(left_high, "u", 3)
+    own_index, exponents, _ = lax.optimization_barrier((u[None], exponents, right_low))
+    own_low, own_high = project(own_index, basis_t, snapshots)
 
     coarse = table(exponents, jnp.arange(COARSE, dtype=jnp.float32) / COARSE)
     fine = table(exponents, jnp.arange(FINE, dtype=jnp.float32) / TIMES)
@@ -440,8 +468,10 @@
         name="gram",
     )(coarse, fine)
 
-    own, solve, terms = lax.optimization_barrier((own, solve, terms))
-    sums = first_sum(at_v, own, [received[s] for s in (1, 2, 3)])
+    own_low, solve, terms = lax.optimization_barrier((own_low, solve, terms))
+    sums = first_sum(
+        at_v, (own_low, relayed_low, direct_low), (own_high, direct_high, relayed_high)
+    )
     received = {s: send(sums[s], "v", s) for s in (2, 1, 3)}
     total = plain_sum(sums[0], [received[s] for s in (1, 2, 3)])
     received = {s: send(total, "w", s) for s in (2, 1, 3)}

time: 99.6 us -> 95.9 us (0.963)
  waiting for transfers between devices: 42 us -> 36.6 us
  starting transfers between devices: 27.7 us -> 30.6 us
  other arithmetic: 1.78 us -> 0.51 us
  local copies, waits for them, and re-layouts: 0.75 us -> 1.75 us
    ppermute x15 -> x18, waiting for transfers between devices: 42 us -> 36.5 us  [send(): return lax.ppermute(value, ('tm', 'space'), shifted(axis, step))]
    ppermute x1, starting transfers between devices: 5.81 us -> 8.36 us  [swap_cores(): lax.ppermute(value, ('tm', 'space'), [(d, d ^ 1) for d in range(128)])]
    mul x2, other arithmetic: 1.6 us -> 0.33 us  [waves(): return (magnitude * jnp.cos(phase_angle), magnitude * jnp.sin(phase_angle))]
    pallas_call x1, Pallas kernels: 1.42 us -> 0.21 us  [first_sum(): pl.pallas_call(first_sum_kernel, in_specs=[pl.BlockSpec(memory_space=pltp...]
    unnamed x24 -> x10, local copies, waits for them, and re-layouts: 0.73 us -> 1.73 us
    ppermute x15 -> x18, starting transfers between devices: 21.9 us -> 22.2 us  [send(): return lax.ppermute(value, ('tm', 'space'), shifted(axis, step))]
  transfers between devices with their start and end apart: 16 -> 19, of which waited for: 12 -> 14; matrix products, arithmetic and copies ran while one was open for 2% -> 1% of each run, Pallas kernels for 18% -> 18%
where the time goes in v3:
time: 95.9 us; the launch traced here: 95.7 us
  waiting for transfers between devices  36.6 us (38%)
  starting transfers between devices  30.6 us (32%)
  Pallas kernels  25.4 us (26%)
  local copies, waits for them, and re-layouts  1.75 us (2%)
    ppermute x18, waiting for transfers between devices, send(): return lax.ppermute(value, ('tm', 'space'), shifted(axis, step))  36.5 us
    ppermute x18, starting transfers between devices, send(): return lax.ppermute(value, ('tm', 'space'), shifted(axis, step))  22.2 us
    pallas_call x3, Pallas kernels, project(): pl.pallas_call(project_kernel, grid_spec=pltpu.PrefetchScalarGridSpec(num...  9.15 us
    ppermute x1, starting transfers between devices, swap_cores(): lax.ppermute(value, ('tm', 'space'), [(d, d ^ 1) for d in range(128)])  8.36 us
    pallas_call x1, Pallas kernels, shards(): pl.pallas_call(gram_kernel, in_specs=[VMEM] * 2, out_specs=[VMEM] * 2, ou...  3.85 us
    pallas_call x1, Pallas kernels, own_residual(): pl.pallas_call(own_kernel, in_specs=[SMEM, VMEM, VMEM, HBM], out_specs=[H...  3.84 us
    pallas_call x1, Pallas kernels, shards(): pl.pallas_call(update_kernel, in_specs=[VMEM] * 4, out_specs=VMEM, out_sh...  3.73 us
    pallas_call x1, Pallas kernels, rest_residual(): pl.pallas_call(rest_kernel, in_specs=[SMEM, VMEM, VMEM, VMEM, VMEM, VMEM,...  3.44 us
  transfers between devices with their start and end apart: 19, of which 14 were waited for; matrix products, arithmetic and copies ran while one was open for 1% of the time, Pallas kernels for 18%

profile of v3, /device:TPU:1, one launch (start us, length us, event | category | flops | bytes accessed | tf_op | source)
XLA Modules:
  0.0 95.7 jit_solution(14247154176789278012)
XLA Ops:
  1.8 2.9 %project.4 = (f32[2,128,512]{2,1,0:T(8,128)}, f32[2,128,512]{2,1,0:T(8,128)}) custom-call(s32[1]{0:T(128)} %bitcast.4.index_ref, bf16[128,512]{1,0:T(8,128)(2,1)S(1)} %get-tuple-element.31.basis_ref, bf16[512,8192]{1,0:T(8,128)(2,1)} %snapshots_ref.7), custom_call_target="tpu_custom_call" | custom-call | flops 268435456 | bytes 3145728 | tf_op jit(solution)/shard_map/project/pallas_call | solution.py:183
  4.7 2.5 %collective-permute-start = (f32[2,128,512]{2,1,0:T(8,128)}, f32[2,128,512]{2,1,0:T(8,128)S(1)}, u32[]{:S(2)}, u32[]{:S(2)}) collective-permute-start(f32[2,128,512]{2,1,0:T(8,128)} %get-tuple-element.34), channel_id=1, source_target_pairs={{0,2},{1,33},{2,4},{3,35},{4,6},{5,37},{6,0},{7,39},{8,10},{9,41},... | collective-permute-start | bytes 1572872 | tf_op jit(solution)/shard_map/ppermute | solution.py:46
  7.1 2.1 %collective-permute-start.1 = (f32[2,128,512]{2,1,0:T(8,128)}, f32[2,128,512]{2,1,0:T(8,128)S(1)}, u32[]{:S(2)}, u32[]{:S(2)}) collective-permute-start(f32[2,128,512]{2,1,0:T(8,128)} %get-tuple-element.35), channel_id=1, source_target_pairs={{0,6},{1,97},{2,0},{3,99},{4,2},{5,101},{6,4},{7,103},{8,14},{9,10... | collective-permute-start | bytes 1572872 | tf_op jit(solution)/shard_map/ppermute | solution.py:46
  9.3 4.2 %project.3 = (f32[2,128,512]{2,1,0:T(8,128)S(1)}, f32[2,128,512]{2,1,0:T(8,128)S(1)}, f32[2,128,512]{2,1,0:T(8,128)}, f32[2,128,512]{2,1,0:T(8,128)}) custom-call(s32[2]{0:T(128)S(1)} %pad_add_fusion.index_ref, bf16[128,512]{1,0:T(8,128)(2,1)S(1)} %get-tuple-element.31.basis_ref, bf16[512,8192]{1,0:T(8,128)(2,1)} %snapshots_ref.7), custom_call_target="tpu_custom_call" | custom-call | flops 536870912 | bytes 6291456 | tf_op jit(solution)/shard_map/project/pallas_call | solution.py:183
  13.6 1.5 %collective-permute-start.3 = (f32[2,128,512]{2,1,0:T(8,128)}, f32[2,128,512]{2,1,0:T(8,128)S(1)}, u32[]{:S(2)}, u32[]{:S(2)}) collective-permute-start(f32[2,128,512]{2,1,0:T(8,128)} %get-tuple-element.45), channel_id=1, source_target_pairs={{0,6},{1,97},{2,0},{3,99},{4,2},{5,101},{6,4},{7,103},{8,14},{9,10... | collective-permute-start | bytes 1572872 | tf_op jit(solution)/shard_map/ppermute | solution.py:46
  15.1 1.2 %collective-permute-done.from_left_ref = f32[2,128,512]{2,1,0:T(8,128)S(1)} collective-permute-done((f32[2,128,512]{2,1,0:T(8,128)}, f32[2,128,512]{2,1,0:T(8,128)S(1)}, u32[]{:S(2)}, u32[]{:S(2)}) %collective-permute-start) | collective-permute-done | bytes 524320 | tf_op jit(solution)/shard_map/ppermute | solution.py:46
  16.3 1.0 %copy-done = f32[2,128,512]{2,1,0:T(8,128)S(1)} copy-done((f32[2,128,512]{2,1,0:T(8,128)S(1)}, f32[2,128,512]{2,1,0:T(8,128)}, u32[]{:S(2)}) %copy-start) | copy-done | bytes 524312
  17.8 1.1 %collective-permute-start.2 = (f32[2,128,512]{2,1,0:T(8,128)S(1)}, f32[2,128,512]{2,1,0:T(8,128)S(1)}, u32[]{:S(2)}, u32[]{:S(2)}) collective-permute-start(f32[2,128,512]{2,1,0:T(8,128)S(1)} %get-tuple-element.36), channel_id=1, source_target_pairs={{0,2},{1,33},{2,4},{3,35},{4,6},{5,37},{6,0},{7,39},{8,10},{9,41},... | collective-permute-start | bytes 1572872 | tf_op jit(solution)/shard_map/ppermute | solution.py:46
  18.9 1.8 %collective-permute-start.5 = (f32[2,128,512]{2,1,0:T(8,128)S(1)}, f32[2,128,512]{2,1,0:T(8,128)S(1)}, u32[]{:S(2)}, u32[]{:S(2)}) collective-permute-start(f32[2,128,512]{2,1,0:T(8,128)S(1)} %get-tuple-element.48), channel_id=1, source_target_pairs={{0,6},{1,97},{2,0},{3,99},{4,2},{5,101},{6,4},{7,103},{8,14},{9,10... | collective-permute-start | bytes 1572872 | tf_op jit(solution)/shard_map/ppermute | solution.py:46
  20.7 2.0 %project.5 = (f32[2,128,512]{2,1,0:T(8,128)S(1)}, f32[2,128,512]{2,1,0:T(8,128)S(1)}) custom-call(s32[1]{0:T(128)} %bitcast.index_ref.u_ref, bf16[128,512]{1,0:T(8,128)(2,1)S(1)} %get-tuple-element.31.basis_ref, bf16[512,8192]{1,0:T(8,128)(2,1)} %snapshots_ref.7), custom_call_target="tpu_custom_call" | custom-call | flops 268435456 | bytes 3145728 | tf_op jit(solution)/shard_map/project/pallas_call | solution.py:183
  22.9 3.9 %gram.1 = (f32[64,64]{1,0:T(8,128)S(1)}, f32[4,32,32]{2,1,0:T(8,128)S(1)}) custom-call(f32[4,32,512]{2,1,0:T(8,128)S(1)} %pad_maximum_fusion.coarse_ref, f32[4,32,256]{2,1,0:T(8,128)S(1)} %pad_maximum_fusion.1.fine_ref), custom_call_target="tpu_custom_call" | custom-call | flops 1073741824 | bytes 16777216 | tf_op jit(solution)/shard_map/gram/pallas_call | solution.py:456
  26.8 0.9 collective-permute-done.5.refs_5_
  27.7 2.5 %collective-permute-done.2.refs_1_ = f32[2,128,512]{2,1,0:T(8,128)S(1)} collective-permute-done((f32[2,128,512]{2,1,0:T(8,128)S(1)}, f32[2,128,512]{2,1,0:T(8,128)S(1)}, u32[]{:S(2)}, u32[]{:S(2)}) %collective-permute-start.2) | collective-permute-done | bytes 524320 | tf_op jit(solution)/shard_map/ppermute | solution.py:46
  30.4 1.0 %collective-permute-start.6 = (f32[128,512]{1,0:T(8,128)S(1)}, f32[128,512]{1,0:T(8,128)S(1)}, u32[]{:S(2)}, u32[]{:S(2)}) collective-permute-start(f32[128,512]{1,0:T(8,128)S(1)} %get-tuple-element.50), channel_id=1, source_target_pairs={{0,8},{1,3},{2,10},{3,5},{4,12},{5,7},{6,14},{7,1},{8,16},{9,11},{... | collective-permute-start | bytes 786440 | tf_op jit(solution)/shard_map/ppermute | solution.py:46
  31.4 2.5 %collective-permute-start.7 = (f32[128,512]{1,0:T(8,128)S(1)}, f32[128,512]{1,0:T(8,128)S(1)}, u32[]{:S(2)}, u32[]{:S(2)}) collective-permute-start(f32[128,512]{1,0:T(8,128)S(1)} %get-tuple-element.51), channel_id=1, source_target_pairs={{0,16},{1,5},{2,18},{3,7},{4,20},{5,1},{6,22},{7,3},{8,24},{9,13},... | collective-permute-start | bytes 786440 | tf_op jit(solution)/shard_map/ppermute | solution.py:46
  33.8 1.1 %collective-permute-start.8 = (f32[128,512]{1,0:T(8,128)S(1)}, f32[128,512]{1,0:T(8,128)S(1)}, u32[]{:S(2)}, u32[]{:S(2)}) collective-permute-start(f32[128,512]{1,0:T(8,128)S(1)} %get-tuple-element.52), channel_id=1, source_target_pairs={{0,24},{1,7},{2,26},{3,1},{4,28},{5,3},{6,30},{7,5},{8,0},{9,15},{... | collective-permute-start | bytes 786440 | tf_op jit(solution)/shard_map/ppermute | solution.py:46
  35.0 2.2 %collective-permute-done.6.r1_ref = f32[128,512]{1,0:T(8,128)S(1)} collective-permute-done((f32[128,512]{1,0:T(8,128)S(1)}, f32[128,512]{1,0:T(8,128)S(1)}, u32[]{:S(2)}, u32[]{:S(2)}) %collective-permute-start.6) | collective-permute-done | bytes 262176 | tf_op jit(solution)/shard_map/ppermute | solution.py:46
  37.2 3.5 %collective-permute-done.7.r2_ref = f32[128,512]{1,0:T(8,128)S(1)} collective-permute-done((f32[128,512]{1,0:T(8,128)S(1)}, f32[128,512]{1,0:T(8,128)S(1)}, u32[]{:S(2)}, u32[]{:S(2)}) %collective-permute-start.7) | collective-permute-done | bytes 262176 | tf_op jit(solution)/shard_map/ppermute | solution.py:46
  40.7 2.7 %collective-permute-start.11 = (f32[128,512]{1,0:T(8,128)S(1)}, f32[128,512]{1,0:T(8,128)S(1)}, u32[]{:S(2)}, u32[]{:S(2)}) collective-permute-start(f32[128,512]{1,0:T(8,128)S(1)} %plain_sum.2.own_ref), channel_id=1, source_target_pairs={{0,96},{1,25},{2,98},{3,27},{4,100},{5,29},{6,102},{7,31},{8,104},... | collective-permute-start | bytes 786440 | tf_op jit(solution)/shard_map/ppermute | solution.py:46
  44.5 5.1 %collective-permute-done.11.r3_ref = f32[128,512]{1,0:T(8,128)S(1)} collective-permute-done((f32[128,512]{1,0:T(8,128)S(1)}, f32[128,512]{1,0:T(8,128)S(1)}, u32[]{:S(2)}, u32[]{:S(2)}) %collective-permute-start.11) | collective-permute-done | bytes 262176 | tf_op jit(solution)/shard_map/ppermute | solution.py:46
  50.3 2.7 %collective-permute-done.9.r1_ref = f32[128,512]{1,0:T(8,128)S(1)} collective-permute-done((f32[128,512]{1,0:T(8,128)S(1)}, f32[128,512]{1,0:T(8,128)S(1)}, u32[]{:S(2)}, u32[]{:S(2)}) %collective-permute-start.9) | collective-permute-done | bytes 262176 | tf_op jit(solution)/shard_map/ppermute | solution.py:46
  53.5 2.5 %collective-permute-start.14 = (f32[64,640]{1,0:T(8,128)S(1)}, f32[64,640]{1,0:T(8,128)S(1)}, u32[]{:S(2)}, u32[]{:S(2)}) collective-permute-start(f32[64,640]{1,0:T(8,128)S(1)} %amplitudes.1.own_ref), channel_id=1, source_target_pairs={{0,24},{1,7},{2,26},{3,1},{4,28},{5,3},{6,30},{7,5},{8,0},{9,15},{... | collective-permute-start | bytes 491528 | tf_op jit(solution)/shard_map/ppermute | solution.py:46
  56.9 3.1 %collective-permute-done.14.r3_ref = f32[64,640]{1,0:T(8,128)S(1)} collective-permute-done((f32[64,640]{1,0:T(8,128)S(1)}, f32[64,640]{1,0:T(8,128)S(1)}, u32[]{:S(2)}, u32[]{:S(2)}) %collective-permute-start.14) | collective-permute-done | bytes 163872 | tf_op jit(solution)/shard_map/ppermute | solution.py:46
  60.1 1.8 %collective-permute-done.13.r2_ref = f32[64,640]{1,0:T(8,128)S(1)} collective-permute-done((f32[64,640]{1,0:T(8,128)S(1)}, f32[64,640]{1,0:T(8,128)S(1)}, u32[]{:S(2)}, u32[]{:S(2)}) %collective-permute-start.13) | collective-permute-done | bytes 163872 | tf_op jit(solution)/shard_map/ppermute | solution.py:46
  61.8 1.7 %collective-permute-done.12.r1_ref = f32[64,640]{1,0:T(8,128)S(1)} collective-permute-done((f32[64,640]{1,0:T(8,128)S(1)}, f32[64,640]{1,0:T(8,128)S(1)}, u32[]{:S(2)}, u32[]{:S(2)}) %collective-permute-start.12) | collective-permute-done | bytes 163872 | tf_op jit(solution)/shard_map/ppermute | solution.py:46
  65.1 3.8 %own_residual.1 = (bf16[512,8192]{1,0:T(8,128)(2,1)}, f32[64,8192]{1,0:T(8,128)}, bf16[3,512,2048]{2,1,0:T(8,128)(2,1)S(1)}) custom-call(s32[1]{0:T(128)} %bitcast.index_ref.u_ref, bf16[512,64]{1,0:T(8,128)(2,1)S(1)} %get-tuple-element.53.basis_ref, f32[64,2176]{1,0:T(8,128)S(1)} %join.1.amp_ref, bf16[512,8192]{1,0:T(8,128)(2,1)S(1)} %bitcast.32), custom_call_target="tpu_custom_call" | custom-call | flops 134217728 | bytes 11534336 | tf_op jit(solution)/shard_map/own_residual/pallas_call | solution.py:373
  68.9 3.0 %collective-permute-done.17.a2 = f32[64,2176]{1,0:T(8,128)S(1)} collective-permute-done((f32[64,2176]{1,0:T(8,128)S(1)}, f32[64,2176]{1,0:T(8,128)S(1)}, u32[]{:S(2)}, u32[]{:S(2)}) %collective-permute-start.17) | collective-permute-done | bytes 557088 | tf_op jit(solution)/shard_map/ppermute | solution.py:46
  72.0 2.0 %collective-permute-done.16.a3 = f32[64,2176]{1,0:T(8,128)S(1)} collective-permute-done((f32[64,2176]{1,0:T(8,128)S(1)}, f32[64,2176]{1,0:T(8,128)S(1)}, u32[]{:S(2)}, u32[]{:S(2)}) %collective-permute-start.16) | collective-permute-done | bytes 557088 | tf_op jit(solution)/shard_map/ppermute | solution.py:46
  73.9 6.2 %collective-permute-done.15.a1 = f32[64,2176]{1,0:T(8,128)S(1)} collective-permute-done((f32[64,2176]{1,0:T(8,128)S(1)}, f32[64,2176]{1,0:T(8,128)S(1)}, u32[]{:S(2)}, u32[]{:S(2)}) %collective-permute-start.15) | collective-permute-done | bytes 557088 | tf_op jit(solution)/shard_map/ppermute | solution.py:46
  80.1 8.4 %collective-permute-start.18 = (f32[64,128]{1,0:T(8,128)S(1)}, f32[64,128]{1,0:T(8,128)S(1)}, u32[]{:S(2)}, u32[]{:S(2)}) collective-permute-start(f32[64,128]{1,0:T(8,128)S(1)} %plain_sum.3.here_ref), channel_id=1, source_target_pairs={{0,1},{1,0},{2,3},{3,2},{4,5},{5,4},{6,7},{7,6},{8,9},{9,8},{10,11... | collective-permute-start | bytes 98312 | tf_op jit(solution)/shard_map/ppermute | solution.py:50
  88.5 3.4 %rest_residual.1 = (bf16[512,8192]{1,0:T(8,128)(2,1)}, f32[64,8192]{1,0:T(8,128)}) custom-call(s32[1]{0:T(128)} %bitcast.index_ref.u_ref, bf16[512,64]{1,0:T(8,128)(2,1)S(1)} %get-tuple-element.53.basis_ref, f32[64,2176]{1,0:T(8,128)S(1)} %collective-permute-done.15.a1, ...), custom_call_target="tpu_custom_call", output_to_operand_aliasing={{0}: (6, {}), {1}: (7, {})} | custom-call | flops 402653184 | bytes 8388608 | tf_op jit(solution)/shard_map/rest_residual/pallas_call | solution.py:392
  91.9 3.7 %update.1 = f32[2,32]{1,0:T(2,128)} custom-call(f32[2,32]{1,0:T(2,128)S(1)} %copy-done.2, f32[4,32,32]{2,1,0:T(8,128)S(1)} %get-tuple-element.42.terms_ref, f32[64,128]{1,0:T(8,128)S(1)} %plain_sum.3.here_ref, f32[64,128]{1,0:T(8,128)S(1)} %collective-permute-done.18.there_ref), custom_call_target="tpu_custom_call" | custom-call | tf_op jit(solution)/shard_map/update/pallas_call | solution.py:490
  (49 shorter events, 6.9 us)
Async XLA Ops:
  0.6 0.7 copy-start.1
  1.8 15.7 %copy-start.2 = (f32[2,32]{1,0:T(2,128)S(1)}, f32[2,32]{1,0:T(2,128)}, u32[]{:S(2)}) copy-start(f32[2,32]{1,0:T(2,128)} %exponents_ref.2) | copy-start | bytes 772
  4.7 11.6 %collective-permute-start = (f32[2,128,512]{2,1,0:T(8,128)}, f32[2,128,512]{2,1,0:T(8,128)S(1)}, u32[]{:S(2)}, u32[]{:S(2)}) collective-permute-start(f32[2,128,512]{2,1,0:T(8,128)} %get-tuple-element.34), channel_id=1, source_target_pairs={{0,2},{1,33},{2,4},{3,35},{4,6},{5,37},{6,0},{7,39},{8,10},{9,41},... | collective-permute-start | bytes 1572872 | tf_op jit(solution)/shard_map/ppermute | solution.py:46
  7.1 9.2 %collective-permute-start.1 = (f32[2,128,512]{2,1,0:T(8,128)}, f32[2,128,512]{2,1,0:T(8,128)S(1)}, u32[]{:S(2)}, u32[]{:S(2)}) collective-permute-start(f32[2,128,512]{2,1,0:T(8,128)} %get-tuple-element.35), channel_id=1, source_target_pairs={{0,6},{1,97},{2,0},{3,99},{4,2},{5,101},{6,4},{7,103},{8,14},{9,10... | collective-permute-start | bytes 1572872 | tf_op jit(solution)/shard_map/ppermute | solution.py:46
  13.6 13.2 %collective-permute-start.3 = (f32[2,128,512]{2,1,0:T(8,128)}, f32[2,128,512]{2,1,0:T(8,128)S(1)}, u32[]{:S(2)}, u32[]{:S(2)}) collective-permute-start(f32[2,128,512]{2,1,0:T(8,128)} %get-tuple-element.45), channel_id=1, source_target_pairs={{0,6},{1,97},{2,0},{3,99},{4,2},{5,101},{6,4},{7,103},{8,14},{9,10... | collective-permute-start | bytes 1572872 | tf_op jit(solution)/shard_map/ppermute | solution.py:46
  15.0 11.8 %collective-permute-start.4 = (f32[2,128,512]{2,1,0:T(8,128)S(1)}, f32[2,128,512]{2,1,0:T(8,128)S(1)}, u32[]{:S(2)}, u32[]{:S(2)}) collective-permute-start(f32[2,128,512]{2,1,0:T(8,128)S(1)} %get-tuple-element.47), channel_id=1, source_target_pairs={{0,2},{1,33},{2,4},{3,35},{4,6},{5,37},{6,0},{7,39},{8,10},{9,41},... | collective-permute-start | bytes 1572872 | tf_op jit(solution)/shard_map/ppermute | solution.py:46
  16.3 1.0 %copy-start = (f32[2,128,512]{2,1,0:T(8,128)S(1)}, f32[2,128,512]{2,1,0:T(8,128)}, u32[]{:S(2)}) copy-start(f32[2,128,512]{2,1,0:T(8,128)} %get-tuple-element.33.high_ref) | copy-start | bytes 1572868
  17.8 12.3 %collective-permute-start.2 = (f32[2,128,512]{2,1,0:T(8,128)S(1)}, f32[2,128,512]{2,1,0:T(8,128)S(1)}, u32[]{:S(2)}, u32[]{:S(2)}) collective-permute-start(f32[2,128,512]{2,1,0:T(8,128)S(1)} %get-tuple-element.36), channel_id=1, source_target_pairs={{0,2},{1,33},{2,4},{3,35},{4,6},{5,37},{6,0},{7,39},{8,10},{9,41},... | collective-permute-start | bytes 1572872 | tf_op jit(solution)/shard_map/ppermute | solution.py:46
  18.9 46.2 %slice-start = ((s8[8388608]{0:T(1024)(128)(4,1)}), s8[4194304]{0:T(1024)(128)(4,1)S(1)}, s32[]{:S(2)}) async-start(s8[8388608]{0:T(1024)(128)(4,1)} %bitcast.31), calls=%async_computation | async-start | bytes 8388608
  18.9 8.8 %collective-permute-start.5 = (f32[2,128,512]{2,1,0:T(8,128)S(1)}, f32[2,128,512]{2,1,0:T(8,128)S(1)}, u32[]{:S(2)}, u32[]{:S(2)}) collective-permute-start(f32[2,128,512]{2,1,0:T(8,128)S(1)} %get-tuple-element.48), channel_id=1, source_target_pairs={{0,6},{1,97},{2,0},{3,99},{4,2},{5,101},{6,4},{7,103},{8,14},{9,10... | collective-permute-start | bytes 1572872 | tf_op jit(solution)/shard_map/ppermute | solution.py:46
  22.9 42.2 %slice-start.1 = ((s8[8388608]{0:T(1024)(128)(4,1)}), s8[4194304]{0:T(1024)(128)(4,1)S(1)}, s32[]{:S(2)}) async-start(s8[8388608]{0:T(1024)(128)(4,1)} %bitcast.31), calls=%async_computation.1 | async-start | bytes 8388608
  30.4 6.8 %collective-permute-start.6 = (f32[128,512]{1,0:T(8,128)S(1)}, f32[128,512]{1,0:T(8,128)S(1)}, u32[]{:S(2)}, u32[]{:S(2)}) collective-permute-start(f32[128,512]{1,0:T(8,128)S(1)} %get-tuple-element.50), channel_id=1, source_target_pairs={{0,8},{1,3},{2,10},{3,5},{4,12},{5,7},{6,14},{7,1},{8,16},{9,11},{... | collective-permute-start | bytes 786440 | tf_op jit(solution)/shard_map/ppermute | solution.py:46
  31.4 9.3 %collective-permute-start.7 = (f32[128,512]{1,0:T(8,128)S(1)}, f32[128,512]{1,0:T(8,128)S(1)}, u32[]{:S(2)}, u32[]{:S(2)}) collective-permute-start(f32[128,512]{1,0:T(8,128)S(1)} %get-tuple-element.51), channel_id=1, source_target_pairs={{0,16},{1,5},{2,18},{3,7},{4,20},{5,1},{6,22},{7,3},{8,24},{9,13},... | collective-permute-start | bytes 786440 | tf_op jit(solution)/shard_map/ppermute | solution.py:46
  33.8 6.9 %collective-permute-start.8 = (f32[128,512]{1,0:T(8,128)S(1)}, f32[128,512]{1,0:T(8,128)S(1)}, u32[]{:S(2)}, u32[]{:S(2)}) collective-permute-start(f32[128,512]{1,0:T(8,128)S(1)} %get-tuple-element.52), channel_id=1, source_target_pairs={{0,24},{1,7},{2,26},{3,1},{4,28},{5,3},{6,30},{7,5},{8,0},{9,15},{... | collective-permute-start | bytes 786440 | tf_op jit(solution)/shard_map/ppermute | solution.py:46
  40.7 8.8 %collective-permute-start.11 = (f32[128,512]{1,0:T(8,128)S(1)}, f32[128,512]{1,0:T(8,128)S(1)}, u32[]{:S(2)}, u32[]{:S(2)}) collective-permute-start(f32[128,512]{1,0:T(8,128)S(1)} %plain_sum.2.own_ref), channel_id=1, source_target_pairs={{0,96},{1,25},{2,98},{3,27},{4,100},{5,29},{6,102},{7,31},{8,104},... | collective-permute-start | bytes 786440 | tf_op jit(solution)/shard_map/ppermute | solution.py:46
  43.4 6.8 %collective-permute-start.10 = (f32[128,512]{1,0:T(8,128)S(1)}, f32[128,512]{1,0:T(8,128)S(1)}, u32[]{:S(2)}, u32[]{:S(2)}) collective-permute-start(f32[128,512]{1,0:T(8,128)S(1)} %plain_sum.2.own_ref), channel_id=1, source_target_pairs={{0,64},{1,17},{2,66},{3,19},{4,68},{5,21},{6,70},{7,23},{8,72},{9,... | collective-permute-start | bytes 786440 | tf_op jit(solution)/shard_map/ppermute | solution.py:46
  43.8 9.2 %collective-permute-start.9 = (f32[128,512]{1,0:T(8,128)S(1)}, f32[128,512]{1,0:T(8,128)S(1)}, u32[]{:S(2)}, u32[]{:S(2)}) collective-permute-start(f32[128,512]{1,0:T(8,128)S(1)} %plain_sum.2.own_ref), channel_id=1, source_target_pairs={{0,32},{1,9},{2,34},{3,11},{4,36},{5,13},{6,38},{7,15},{8,40},{9,1... | collective-permute-start | bytes 786440 | tf_op jit(solution)/shard_map/ppermute | solution.py:46
  53.5 6.5 %collective-permute-start.14 = (f32[64,640]{1,0:T(8,128)S(1)}, f32[64,640]{1,0:T(8,128)S(1)}, u32[]{:S(2)}, u32[]{:S(2)}) collective-permute-start(f32[64,640]{1,0:T(8,128)S(1)} %amplitudes.1.own_ref), channel_id=1, source_target_pairs={{0,24},{1,7},{2,26},{3,1},{4,28},{5,3},{6,30},{7,5},{8,0},{9,15},{... | collective-permute-start | bytes 491528 | tf_op jit(solution)/shard_map/ppermute | solution.py:46
  56.1 5.8 %collective-permute-start.13 = (f32[64,640]{1,0:T(8,128)S(1)}, f32[64,640]{1,0:T(8,128)S(1)}, u32[]{:S(2)}, u32[]{:S(2)}) collective-permute-start(f32[64,640]{1,0:T(8,128)S(1)} %amplitudes.1.own_ref), channel_id=1, source_target_pairs={{0,16},{1,5},{2,18},{3,7},{4,20},{5,1},{6,22},{7,3},{8,24},{9,13},... | collective-permute-start | bytes 491528 | tf_op jit(solution)/shard_map/ppermute | solution.py:46
  56.9 6.6 %collective-permute-start.12 = (f32[64,640]{1,0:T(8,128)S(1)}, f32[64,640]{1,0:T(8,128)S(1)}, u32[]{:S(2)}, u32[]{:S(2)}) collective-permute-start(f32[64,640]{1,0:T(8,128)S(1)} %amplitudes.1.own_ref), channel_id=1, source_target_pairs={{0,8},{1,3},{2,10},{3,5},{4,12},{5,7},{6,14},{7,1},{8,16},{9,11},{... | collective-permute-start | bytes 491528 | tf_op jit(solution)/shard_map/ppermute | solution.py:46
  63.5 8.5 %collective-permute-start.17 = (f32[64,2176]{1,0:T(8,128)S(1)}, f32[64,2176]{1,0:T(8,128)S(1)}, u32[]{:S(2)}, u32[]{:S(2)}) collective-permute-start(f32[64,2176]{1,0:T(8,128)S(1)} %join.1.amp_ref), channel_id=1, source_target_pairs={{0,6},{1,97},{2,0},{3,99},{4,2},{5,101},{6,4},{7,103},{8,14},{9,10... | collective-permute-start | bytes 1671176 | tf_op jit(solution)/shard_map/ppermute | solution.py:46
  63.9 10.0 %collective-permute-start.16 = (f32[64,2176]{1,0:T(8,128)S(1)}, f32[64,2176]{1,0:T(8,128)S(1)}, u32[]{:S(2)}, u32[]{:S(2)}) collective-permute-start(f32[64,2176]{1,0:T(8,128)S(1)} %join.1.amp_ref), channel_id=1, source_target_pairs={{0,4},{1,65},{2,6},{3,67},{4,0},{5,69},{6,2},{7,71},{8,12},{9,73},... | collective-permute-start | bytes 1671176 | tf_op jit(solution)/shard_map/ppermute | solution.py:46
  64.2 15.9 %collective-permute-start.15 = (f32[64,2176]{1,0:T(8,128)S(1)}, f32[64,2176]{1,0:T(8,128)S(1)}, u32[]{:S(2)}, u32[]{:S(2)}) collective-permute-start(f32[64,2176]{1,0:T(8,128)S(1)} %join.1.amp_ref), channel_id=1, source_target_pairs={{0,2},{1,33},{2,4},{3,35},{4,6},{5,37},{6,0},{7,39},{8,10},{9,41},... | collective-permute-start | bytes 1671176 | tf_op jit(solution)/shard_map/ppermute | solution.py:46
  80.1 11.8 %collective-permute-start.18 = (f32[64,128]{1,0:T(8,128)S(1)}, f32[64,128]{1,0:T(8,128)S(1)}, u32[]{:S(2)}, u32[]{:S(2)}) collective-permute-start(f32[64,128]{1,0:T(8,128)S(1)} %plain_sum.3.here_ref), channel_id=1, source_target_pairs={{0,1},{1,0},{2,3},{3,2},{4,5},{5,4},{6,7},{7,6},{8,9},{9,8},{10,11... | collective-permute-start | bytes 98312 | tf_op jit(solution)/shard_map/ppermute | solution.py:50

commit v4 on v3

--- a/solution.py
+++ b/solution.py
@@ -1,3 +1,5 @@
+import functools
+
 import jax
 import jax.numpy as jnp
 from jax import lax
@@ -19,7 +21,7 @@
 EXACT = lax.Precision.HIGHEST
 VMEM = pl.BlockSpec(memory_space=pltpu.VMEM)
 PARAMS = pltpu.CompilerParams(vmem_limit_bytes=24 * 1024 * 1024)
-WIDE_PARAMS = pltpu.CompilerParams(vmem_limit_bytes=52 * 1024 * 1024)
+WIDE_PARAMS = pltpu.CompilerParams(vmem_limit_bytes=46 * 1024 * 1024)
 AXES = {"u": "xz", "v": "yx", "w": "zy"}
 
 
@@ -111,17 +113,31 @@
 
 def eliminate(real, imag, size):
     row_index = lax.broadcasted_iota(jnp.int32, real.shape, 0)
-    for k in range(size):
-        inverse_pivot = 1.0 / real[k : k + 1, k : k + 1]
-        row_real = real[k : k + 1, :] * inverse_pivot
-        row_imag = imag[k : k + 1, :] * inverse_pivot
-        col_real = real[:, k : k + 1]
-        col_imag = imag[:, k : k + 1]
-        next_real = real - (col_real * row_real - col_imag * row_imag)
-        next_imag = imag - (col_real * row_imag + col_imag * row_real)
-        here = row_index == k
-        real = jnp.where(here, row_real, next_real)
-        imag = jnp.where(here, row_imag, next_imag)
+    wide = (1, real.shape[1])
+    for k in range(0, size, 2):
+        upper, lower = slice(k, k + 1), slice(k + 1, k + 2)
+        inverse_a = 1.0 / jnp.broadcast_to(real[upper, upper], wide)
+        b = jnp.broadcast_to(real[lower, lower], wide)
+        c_real = jnp.broadcast_to(real[upper, lower], wide)
+        c_imag = jnp.broadcast_to(imag[upper, lower], wide)
+        l_real = jnp.broadcast_to(real[lower, upper], wide) * inverse_a
+        l_imag = jnp.broadcast_to(imag[lower, upper], wide) * inverse_a
+        inverse_s = 1.0 / (b - (l_real * c_real - l_imag * c_imag))
+        r1, i1, r2, i2 = real[upper], imag[upper], real[lower], imag[lower]
+        r2, i2 = (
+            (r2 - (l_real * r1 - l_imag * i1)) * inverse_s,
+            (i2 - (l_real * i1 + l_imag * r1)) * inverse_s,
+        )
+        r1, i1 = (
+            (r1 - (c_real * r2 - c_imag * i2)) * inverse_a,
+            (i1 - (c_real * i2 + c_imag * r2)) * inverse_a,
+        )
+        p_real, p_imag = real[:, upper], imag[:, upper]
+        q_real, q_imag = real[:, lower], imag[:, lower]
+        next_real = real - ((p_real * r1 - p_imag * i1) + (q_real * r2 - q_imag * i2))
+        next_imag = imag - ((p_real * i1 + p_imag * r1) + (q_real * i2 + q_imag * r2))
+        real = jnp.where(row_index == k, r1, jnp.where(row_index == k + 1, r2, next_real))
+        imag = jnp.where(row_index == k, i1, jnp.where(row_index == k + 1, i2, next_imag))
     return real, imag
 
 
@@ -340,21 +356,24 @@
     store.wait()
 
 
-def rest_kernel(u_ref, basis_ref, a1, a2, a3, rest_ref, k1, k2, residual_ref, amp_out_ref, new, sems):
+def rest_kernel(places, u_ref, basis_ref, rest_ref, *refs):
+    count = len(places)
+    amp_refs = refs[:count]
+    residual_ref, amp_out_ref, new, sems = refs[-4:]
     copies = []
-    for n, (step, amp_ref) in enumerate(zip(ORDER, (a1, a2, a3))):
-        there = columns_of((u_ref[0] - step) & 3)
+    for n, at in enumerate(places):
+        there = columns_of((u_ref[0] - ORDER[at]) & 3)
         copies.append(
             pltpu.make_async_copy(
-                amp_ref.at[:, pl.ds(0, QUARTER)], amp_out_ref.at[:, there], sems.at[n]
+                amp_refs[n].at[:, pl.ds(0, QUARTER)], amp_out_ref.at[:, there], sems.at[n]
             )
         )
         copies[-1].start()
-    for n, (step, amp_ref) in enumerate(zip(ORDER, (a1, a2, a3))):
-        there = columns_of((u_ref[0] - step) & 3)
-        fit_piece(basis_ref, amp_ref, rest_ref.at[n], new.at[n])
+    for n, at in enumerate(places):
+        there = columns_of((u_ref[0] - ORDER[at]) & 3)
+        fit_piece(basis_ref, amp_refs[n], rest_ref.at[at], new.at[n])
         copies.append(
-            pltpu.make_async_copy(new.at[n], residual_ref.at[:, there], sems.at[3 + n])
+            pltpu.make_async_copy(new.at[n], residual_ref.at[:, there], sems.at[count + n])
         )
         copies[-1].start()
     for copy in copies:
@@ -388,23 +407,24 @@
     )(u, basis, amp, snapshots)
 
 
-def rest_residual(u, basis, amps, rest, residual, amp_out):
-    return pl.pallas_call(
-        rest_kernel,
-        in_specs=[SMEM, VMEM, VMEM, VMEM, VMEM, VMEM, HBM, HBM],
+def rest_residual(places, u, basis, rest, amps, residual, amp_out):
+    count = len(places)
+    return pl.pallas_call(
+        functools.partial(rest_kernel, places),
+        in_specs=[SMEM] + [VMEM] * (2 + count) + [HBM, HBM],
         out_specs=[HBM, HBM],
         out_shape=RESULTS,
-        input_output_aliases={6: 0, 7: 1},
+        input_output_aliases={3 + count: 0, 4 + count: 1},
         scratch_shapes=[
-            pltpu.VMEM((3, ROWS, QUARTER), jnp.bfloat16),
-            pltpu.SemaphoreType.DMA((6,)),
+            pltpu.VMEM((count, ROWS, QUARTER), jnp.bfloat16),
+            pltpu.SemaphoreType.DMA((2 * count,)),
         ],
         compiler_params=PARAMS,
         cost_estimate=pl.CostEstimate(
-            flops=6 * 64 * ROWS * QUARTER, bytes_accessed=8 << 20, transcendentals=0
+            flops=2 * count * 64 * ROWS * QUARTER, bytes_accessed=count * (5 << 19), transcendentals=0
         ),
         name="rest_residual",
-    )(u, basis, *amps, rest, residual, amp_out)
+    )(u, basis, rest, *amps, residual, amp_out)
 
 
 def update_kernel(exponents_ref, terms_ref, here_ref, there_ref, out_ref):
@@ -480,12 +500,15 @@
     amp = join(at_v, amp, [received[s] for s in (1, 2, 3)])
     received = {s: send(amp, "u", s) for s in (2, 1, 3)}
     residual, amp_out, rest = own_residual(u[None], basis, amp, snapshots)
-    sums = plain_sum(
-        amp[:, QUARTER:], [received[s][:, QUARTER:] for s in (1, 2, 3)]
-    )
+    residual, amp_out = rest_residual(
+        (1, 2), u[None], basis, rest, [received[3], received[2]], residual, amp_out
+    )
+    ends = [received[s][:, QUARTER:] for s in (1, 2, 3)]
+    ends[2], residual = lax.optimization_barrier((ends[2], residual))
+    sums = plain_sum(amp[:, QUARTER:], ends)
     other = swap_cores(sums)
     residual, amp_out = rest_residual(
-        u[None], basis, [received[step] for step in ORDER], rest, residual, amp_out
+        (0,), u[None], basis, rest, [received[1]], residual, amp_out
     )
     new_exponents = pl.pallas_call(
         update_kernel,

time: 95.9 us -> 89.8 us (0.936)
  waiting for transfers between devices: 36.6 us -> 30.8 us
  local copies, waits for them, and re-layouts: 1.75 us -> 0.71 us
    ppermute x18, waiting for transfers between devices: 36.5 us -> 30.8 us  [send(): return lax.ppermute(value, ('tm', 'space'), shifted(axis, step))]
    ppermute x18, starting transfers between devices: 22.2 us -> 23.7 us  [send(): return lax.ppermute(value, ('tm', 'space'), shifted(axis, step))]
    pallas_call x1 -> x2, Pallas kernels: 3.44 us -> 4.81 us  [rest_residual(): pl.pallas_call(functools.partial(rest_kernel, places), in_specs=[SMEM] +...]
    unnamed x10 -> x8, local copies, waits for them, and re-layouts: 1.73 us -> 0.7 us
  transfers between devices with their start and end apart: 19 -> 19, of which waited for: 14 -> 13; matrix products, arithmetic and copies ran while one was open for 1% -> 1% of each run, Pallas kernels for 18% -> 20%
where the time goes in v4:
time: 89.8 us; the launch traced here: 89.7 us
  starting transfers between devices  31.4 us (35%)
  waiting for transfers between devices  30.8 us (34%)
  Pallas kernels  25.3 us (28%)
    ppermute x18, waiting for transfers between devices, send(): return lax.ppermute(value, ('tm', 'space'), shifted(axis, step))  30.8 us
    ppermute x18, starting transfers between devices, send(): return lax.ppermute(value, ('tm', 'space'), shifted(axis, step))  23.7 us
    pallas_call x3, Pallas kernels, project(): pl.pallas_call(project_kernel, grid_spec=pltpu.PrefetchScalarGridSpec(num...  9.31 us
    ppermute x1, starting transfers between devices, swap_cores(): lax.ppermute(value, ('tm', 'space'), [(d, d ^ 1) for d in range(128)])  7.64 us
    pallas_call x2, Pallas kernels, rest_residual(): pl.pallas_call(functools.partial(rest_kernel, places), in_specs=[SMEM] +...  4.81 us
    pallas_call x1, Pallas kernels, own_residual(): pl.pallas_call(own_kernel, in_specs=[SMEM, VMEM, VMEM, HBM], out_specs=[H...  3.84 us
    pallas_call x1, Pallas kernels, shards(): pl.pallas_call(gram_kernel, in_specs=[VMEM] * 2, out_specs=[VMEM] * 2, ou...  3.03 us
    pallas_call x1, Pallas kernels, shards(): pl.pallas_call(update_kernel, in_specs=[VMEM] * 4, out_specs=VMEM, out_sh...  2.95 us
  transfers between devices with their start and end apart: 19, of which 13 were waited for; matrix products, arithmetic and copies ran while one was open for 1% of the time, Pallas kernels for 20%

profile of v4, /device:TPU:1, one launch (start us, length us, event | category | flops | bytes accessed | tf_op | source)
XLA Modules:
  0.0 89.7 jit_solution(17020689519482103355)
XLA Ops:
  1.8 2.9 %project.4 = (f32[2,128,512]{2,1,0:T(8,128)}, f32[2,128,512]{2,1,0:T(8,128)}) custom-call(s32[1]{0:T(128)} %bitcast.4.index_ref, bf16[128,512]{1,0:T(8,128)(2,1)S(1)} %get-tuple-element.35.basis_ref, bf16[512,8192]{1,0:T(8,128)(2,1)} %snapshots_ref.7), custom_call_target="tpu_custom_call" | custom-call | flops 268435456 | bytes 3145728 | tf_op jit(solution)/shard_map/project/pallas_call | solution.py:199
  4.7 2.5 %collective-permute-start = (f32[2,128,512]{2,1,0:T(8,128)}, f32[2,128,512]{2,1,0:T(8,128)S(1)}, u32[]{:S(2)}, u32[]{:S(2)}) collective-permute-start(f32[2,128,512]{2,1,0:T(8,128)} %get-tuple-element.38), channel_id=1, source_target_pairs={{0,2},{1,33},{2,4},{3,35},{4,6},{5,37},{6,0},{7,39},{8,10},{9,41},... | collective-permute-start | bytes 1572872 | tf_op jit(solution)/shard_map/ppermute | solution.py:48
  7.1 2.1 %collective-permute-start.1 = (f32[2,128,512]{2,1,0:T(8,128)}, f32[2,128,512]{2,1,0:T(8,128)S(1)}, u32[]{:S(2)}, u32[]{:S(2)}) collective-permute-start(f32[2,128,512]{2,1,0:T(8,128)} %get-tuple-element.39), channel_id=1, source_target_pairs={{0,6},{1,97},{2,0},{3,99},{4,2},{5,101},{6,4},{7,103},{8,14},{9,10... | collective-permute-start | bytes 1572872 | tf_op jit(solution)/shard_map/ppermute | solution.py:48
  9.3 4.2 %project.3 = (f32[2,128,512]{2,1,0:T(8,128)S(1)}, f32[2,128,512]{2,1,0:T(8,128)}, f32[2,128,512]{2,1,0:T(8,128)}, f32[2,128,512]{2,1,0:T(8,128)S(1)}) custom-call(s32[2]{0:T(128)S(1)} %pad_add_fusion.index_ref, bf16[128,512]{1,0:T(8,128)(2,1)S(1)} %get-tuple-element.35.basis_ref, bf16[512,8192]{1,0:T(8,128)(2,1)} %snapshots_ref.7), custom_call_target="tpu_custom_call" | custom-call | flops 536870912 | bytes 6291456 | tf_op jit(solution)/shard_map/project/pallas_call | solution.py:199
  13.5 1.5 %collective-permute-start.3 = (f32[2,128,512]{2,1,0:T(8,128)}, f32[2,128,512]{2,1,0:T(8,128)S(1)}, u32[]{:S(2)}, u32[]{:S(2)}) collective-permute-start(f32[2,128,512]{2,1,0:T(8,128)} %get-tuple-element.49), channel_id=1, source_target_pairs={{0,6},{1,97},{2,0},{3,99},{4,2},{5,101},{6,4},{7,103},{8,14},{9,10... | collective-permute-start | bytes 1572872 | tf_op jit(solution)/shard_map/ppermute | solution.py:48
  15.1 1.3 %collective-permute-done.from_left_ref = f32[2,128,512]{2,1,0:T(8,128)S(1)} collective-permute-done((f32[2,128,512]{2,1,0:T(8,128)}, f32[2,128,512]{2,1,0:T(8,128)S(1)}, u32[]{:S(2)}, u32[]{:S(2)}) %collective-permute-start) | collective-permute-done | bytes 524320 | tf_op jit(solution)/shard_map/ppermute | solution.py:48
  16.8 1.1 %collective-permute-start.2 = (f32[2,128,512]{2,1,0:T(8,128)S(1)}, f32[2,128,512]{2,1,0:T(8,128)S(1)}, u32[]{:S(2)}, u32[]{:S(2)}) collective-permute-start(f32[2,128,512]{2,1,0:T(8,128)S(1)} %get-tuple-element.40), channel_id=1, source_target_pairs={{0,2},{1,33},{2,4},{3,35},{4,6},{5,37},{6,0},{7,39},{8,10},{9,41},... | collective-permute-start | bytes 1572872 | tf_op jit(solution)/shard_map/ppermute | solution.py:48
  17.9 2.2 %project.5 = (f32[2,128,512]{2,1,0:T(8,128)S(1)}, f32[2,128,512]{2,1,0:T(8,128)S(1)}) custom-call(s32[1]{0:T(128)} %bitcast.index_ref.u_ref, bf16[128,512]{1,0:T(8,128)(2,1)S(1)} %get-tuple-element.35.basis_ref, bf16[512,8192]{1,0:T(8,128)(2,1)} %snapshots_ref.7), custom_call_target="tpu_custom_call" | custom-call | flops 268435456 | bytes 3145728 | tf_op jit(solution)/shard_map/project/pallas_call | solution.py:199
  20.1 1.8 %collective-permute-start.5 = (f32[2,128,512]{2,1,0:T(8,128)S(1)}, f32[2,128,512]{2,1,0:T(8,128)S(1)}, u32[]{:S(2)}, u32[]{:S(2)}) collective-permute-start(f32[2,128,512]{2,1,0:T(8,128)S(1)} %get-tuple-element.52), channel_id=1, source_target_pairs={{0,6},{1,97},{2,0},{3,99},{4,2},{5,101},{6,4},{7,103},{8,14},{9,10... | collective-permute-start | bytes 1572872 | tf_op jit(solution)/shard_map/ppermute | solution.py:48
  22.0 3.0 %gram.1 = (f32[64,64]{1,0:T(8,128)S(1)}, f32[4,32,32]{2,1,0:T(8,128)S(1)}) custom-call(f32[4,32,512]{2,1,0:T(8,128)S(1)} %pad_maximum_fusion.coarse_ref, f32[4,32,256]{2,1,0:T(8,128)S(1)} %pad_maximum_fusion.1.fine_ref), custom_call_target="tpu_custom_call" | custom-call | flops 1073741824 | bytes 16777216 | tf_op jit(solution)/shard_map/gram/pallas_call | solution.py:476
  25.1 5.3 %collective-permute-done.2.refs_1_ = f32[2,128,512]{2,1,0:T(8,128)S(1)} collective-permute-done((f32[2,128,512]{2,1,0:T(8,128)S(1)}, f32[2,128,512]{2,1,0:T(8,128)S(1)}, u32[]{:S(2)}, u32[]{:S(2)}) %collective-permute-start.2) | collective-permute-done | bytes 524320 | tf_op jit(solution)/shard_map/ppermute | solution.py:48
  30.6 1.0 %collective-permute-start.6 = (f32[128,512]{1,0:T(8,128)S(1)}, f32[128,512]{1,0:T(8,128)S(1)}, u32[]{:S(2)}, u32[]{:S(2)}) collective-permute-start(f32[128,512]{1,0:T(8,128)S(1)} %get-tuple-element.54), channel_id=1, source_target_pairs={{0,8},{1,3},{2,10},{3,5},{4,12},{5,7},{6,14},{7,1},{8,16},{9,11},{... | collective-permute-start | bytes 786440 | tf_op jit(solution)/shard_map/ppermute | solution.py:48
  31.6 2.7 %collective-permute-start.7 = (f32[128,512]{1,0:T(8,128)S(1)}, f32[128,512]{1,0:T(8,128)S(1)}, u32[]{:S(2)}, u32[]{:S(2)}) collective-permute-start(f32[128,512]{1,0:T(8,128)S(1)} %get-tuple-element.55), channel_id=1, source_target_pairs={{0,16},{1,5},{2,18},{3,7},{4,20},{5,1},{6,22},{7,3},{8,24},{9,13},... | collective-permute-start | bytes 786440 | tf_op jit(solution)/shard_map/ppermute | solution.py:48
  35.2 2.2 %collective-permute-done.6.r1_ref = f32[128,512]{1,0:T(8,128)S(1)} collective-permute-done((f32[128,512]{1,0:T(8,128)S(1)}, f32[128,512]{1,0:T(8,128)S(1)}, u32[]{:S(2)}, u32[]{:S(2)}) %collective-permute-start.6) | collective-permute-done | bytes 262176 | tf_op jit(solution)/shard_map/ppermute | solution.py:48
  37.4 3.8 %collective-permute-done.7.r2_ref = f32[128,512]{1,0:T(8,128)S(1)} collective-permute-done((f32[128,512]{1,0:T(8,128)S(1)}, f32[128,512]{1,0:T(8,128)S(1)}, u32[]{:S(2)}, u32[]{:S(2)}) %collective-permute-start.7) | collective-permute-done | bytes 262176 | tf_op jit(solution)/shard_map/ppermute | solution.py:48
  41.2 2.7 %collective-permute-start.10 = (f32[128,512]{1,0:T(8,128)S(1)}, f32[128,512]{1,0:T(8,128)S(1)}, u32[]{:S(2)}, u32[]{:S(2)}) collective-permute-start(f32[128,512]{1,0:T(8,128)S(1)} %plain_sum.2.own_ref), channel_id=1, source_target_pairs={{0,64},{1,17},{2,66},{3,19},{4,68},{5,21},{6,70},{7,23},{8,72},{9,... | collective-permute-start | bytes 786440 | tf_op jit(solution)/shard_map/ppermute | solution.py:48
  45.4 2.6 %collective-permute-done.10.r2_ref = f32[128,512]{1,0:T(8,128)S(1)} collective-permute-done((f32[128,512]{1,0:T(8,128)S(1)}, f32[128,512]{1,0:T(8,128)S(1)}, u32[]{:S(2)}, u32[]{:S(2)}) %collective-permute-start.10) | collective-permute-done | bytes 262176 | tf_op jit(solution)/shard_map/ppermute | solution.py:48
  48.0 3.2 %collective-permute-done.11.r3_ref = f32[128,512]{1,0:T(8,128)S(1)} collective-permute-done((f32[128,512]{1,0:T(8,128)S(1)}, f32[128,512]{1,0:T(8,128)S(1)}, u32[]{:S(2)}, u32[]{:S(2)}) %collective-permute-start.11) | collective-permute-done | bytes 262176 | tf_op jit(solution)/shard_map/ppermute | solution.py:48
  52.0 1.4 %collective-permute-start.12 = (f32[64,640]{1,0:T(8,128)S(1)}, f32[64,640]{1,0:T(8,128)S(1)}, u32[]{:S(2)}, u32[]{:S(2)}) collective-permute-start(f32[64,640]{1,0:T(8,128)S(1)} %amplitudes.1.own_ref), channel_id=1, source_target_pairs={{0,8},{1,3},{2,10},{3,5},{4,12},{5,7},{6,14},{7,1},{8,16},{9,11},{... | collective-permute-start | bytes 491528 | tf_op jit(solution)/shard_map/ppermute | solution.py:48
  53.4 1.6 %collective-permute-start.13 = (f32[64,640]{1,0:T(8,128)S(1)}, f32[64,640]{1,0:T(8,128)S(1)}, u32[]{:S(2)}, u32[]{:S(2)}) collective-permute-start(f32[64,640]{1,0:T(8,128)S(1)} %amplitudes.1.own_ref), channel_id=1, source_target_pairs={{0,16},{1,5},{2,18},{3,7},{4,20},{5,1},{6,22},{7,3},{8,24},{9,13},... | collective-permute-start | bytes 491528 | tf_op jit(solution)/shard_map/ppermute | solution.py:48
  55.1 1.2 %collective-permute-start.14 = (f32[64,640]{1,0:T(8,128)S(1)}, f32[64,640]{1,0:T(8,128)S(1)}, u32[]{:S(2)}, u32[]{:S(2)}) collective-permute-start(f32[64,640]{1,0:T(8,128)S(1)} %amplitudes.1.own_ref), channel_id=1, source_target_pairs={{0,24},{1,7},{2,26},{3,1},{4,28},{5,3},{6,30},{7,5},{8,0},{9,15},{... | collective-permute-start | bytes 491528 | tf_op jit(solution)/shard_map/ppermute | solution.py:48
  56.2 1.2 %collective-permute-done.12.r1_ref = f32[64,640]{1,0:T(8,128)S(1)} collective-permute-done((f32[64,640]{1,0:T(8,128)S(1)}, f32[64,640]{1,0:T(8,128)S(1)}, u32[]{:S(2)}, u32[]{:S(2)}) %collective-permute-start.12) | collective-permute-done | bytes 163872 | tf_op jit(solution)/shard_map/ppermute | solution.py:48
  57.5 2.0 %collective-permute-done.13.r2_ref = f32[64,640]{1,0:T(8,128)S(1)} collective-permute-done((f32[64,640]{1,0:T(8,128)S(1)}, f32[64,640]{1,0:T(8,128)S(1)}, u32[]{:S(2)}, u32[]{:S(2)}) %collective-permute-start.13) | collective-permute-done | bytes 163872 | tf_op jit(solution)/shard_map/ppermute | solution.py:48
  59.8 1.2 %collective-permute-start.17 = (f32[64,2176]{1,0:T(8,128)S(1)}, f32[64,2176]{1,0:T(8,128)S(1)}, u32[]{:S(2)}, u32[]{:S(2)}) collective-permute-start(f32[64,2176]{1,0:T(8,128)S(1)} %join.1.amp_ref), channel_id=1, source_target_pairs={{0,6},{1,97},{2,0},{3,99},{4,2},{5,101},{6,4},{7,103},{8,14},{9,10... | collective-permute-start | bytes 1671176 | tf_op jit(solution)/shard_map/ppermute | solution.py:48
  61.7 3.8 %own_residual.1 = (bf16[512,8192]{1,0:T(8,128)(2,1)}, f32[64,8192]{1,0:T(8,128)}, bf16[3,512,2048]{2,1,0:T(8,128)(2,1)S(1)}) custom-call(s32[1]{0:T(128)} %bitcast.index_ref.u_ref, bf16[512,64]{1,0:T(8,128)(2,1)S(1)} %get-tuple-element.57.basis_ref, f32[64,2176]{1,0:T(8,128)S(1)} %join.1.amp_ref, bf16[512,8192]{1,0:T(8,128)(2,1)S(1)} %bitcast.32), custom_call_target="tpu_custom_call" | custom-call | flops 134217728 | bytes 11534336 | tf_op jit(solution)/shard_map/own_residual/pallas_call | solution.py:392
  65.6 2.7 %collective-permute-done.17.refs_0_ = f32[64,2176]{1,0:T(8,128)S(1)} collective-permute-done((f32[64,2176]{1,0:T(8,128)S(1)}, f32[64,2176]{1,0:T(8,128)S(1)}, u32[]{:S(2)}, u32[]{:S(2)}) %collective-permute-start.17) | collective-permute-done | bytes 557088 | tf_op jit(solution)/shard_map/ppermute | solution.py:48
  68.3 2.7 %collective-permute-done.16.refs_1_ = f32[64,2176]{1,0:T(8,128)S(1)} collective-permute-done((f32[64,2176]{1,0:T(8,128)S(1)}, f32[64,2176]{1,0:T(8,128)S(1)}, u32[]{:S(2)}, u32[]{:S(2)}) %collective-permute-start.16) | collective-permute-done | bytes 557088 | tf_op jit(solution)/shard_map/ppermute | solution.py:48
  71.0 2.7 %rest_residual.2 = (bf16[512,8192]{1,0:T(8,128)(2,1)}, f32[64,8192]{1,0:T(8,128)}) custom-call(s32[1]{0:T(128)} %bitcast.index_ref.u_ref, bf16[512,64]{1,0:T(8,128)(2,1)S(1)} %get-tuple-element.57.basis_ref, bf16[3,512,2048]{2,1,0:T(8,128)(2,1)S(1)} %get-tuple-element.58.rest_ref, ...), custom_call_target="tpu_custom_call", output_to_operand_aliasing={{0}: (5, {}), {1}: (6, {})} | custom-call | flops 268435456 | bytes 5242880 | tf_op jit(solution)/shard_map/rest_residual/pallas_call | solution.py:412
  73.8 3.2 %collective-permute-done.15.refs_0_ = f32[64,2176]{1,0:T(8,128)S(1)} collective-permute-done((f32[64,2176]{1,0:T(8,128)S(1)}, f32[64,2176]{1,0:T(8,128)S(1)}, u32[]{:S(2)}, u32[]{:S(2)}) %collective-permute-start.15) | collective-permute-done | bytes 557088 | tf_op jit(solution)/shard_map/ppermute | solution.py:48
  77.0 7.6 %collective-permute-start.18 = (f32[64,128]{1,0:T(8,128)S(1)}, f32[64,128]{1,0:T(8,128)S(1)}, u32[]{:S(2)}, u32[]{:S(2)}) collective-permute-start(f32[64,128]{1,0:T(8,128)S(1)} %plain_sum.3.here_ref), channel_id=1, source_target_pairs={{0,1},{1,0},{2,3},{3,2},{4,5},{5,4},{6,7},{7,6},{8,9},{9,8},{10,11... | collective-permute-start | bytes 98312 | tf_op jit(solution)/shard_map/ppermute | solution.py:52
  84.6 2.1 %rest_residual.3 = (bf16[512,8192]{1,0:T(8,128)(2,1)}, f32[64,8192]{1,0:T(8,128)}) custom-call(s32[1]{0:T(128)} %bitcast.index_ref.u_ref, bf16[512,64]{1,0:T(8,128)(2,1)S(1)} %get-tuple-element.57.basis_ref, bf16[3,512,2048]{2,1,0:T(8,128)(2,1)S(1)} %get-tuple-element.58.rest_ref, ...), custom_call_target="tpu_custom_call", output_to_operand_aliasing={{0}: (4, {}), {1}: (5, {})} | custom-call | flops 134217728 | bytes 2621440 | tf_op jit(solution)/shard_map/rest_residual/pallas_call | solution.py:412
  86.7 2.9 %update.1 = f32[2,32]{1,0:T(2,128)} custom-call(f32[2,32]{1,0:T(2,128)S(1)} %copy-done.1, f32[4,32,32]{2,1,0:T(8,128)S(1)} %get-tuple-element.46.terms_ref, f32[64,128]{1,0:T(8,128)S(1)} %plain_sum.3.here_ref, f32[64,128]{1,0:T(8,128)S(1)} %collective-permute-done.18.there_ref), custom_call_target="tpu_custom_call" | custom-call | tf_op jit(solution)/shard_map/update/pallas_call | solution.py:513
  (48 shorter events, 6.2 us)
Async XLA Ops:
  0.6 0.7 copy-start
  1.8 14.7 %copy-start.1 = (f32[2,32]{1,0:T(2,128)S(1)}, f32[2,32]{1,0:T(2,128)}, u32[]{:S(2)}) copy-start(f32[2,32]{1,0:T(2,128)} %exponents_ref.2) | copy-start | bytes 772
  4.7 11.6 %collective-permute-start = (f32[2,128,512]{2,1,0:T(8,128)}, f32[2,128,512]{2,1,0:T(8,128)S(1)}, u32[]{:S(2)}, u32[]{:S(2)}) collective-permute-start(f32[2,128,512]{2,1,0:T(8,128)} %get-tuple-element.38), channel_id=1, source_target_pairs={{0,2},{1,33},{2,4},{3,35},{4,6},{5,37},{6,0},{7,39},{8,10},{9,41},... | collective-permute-start | bytes 1572872 | tf_op jit(solution)/shard_map/ppermute | solution.py:48
  7.1 9.2 %collective-permute-start.1 = (f32[2,128,512]{2,1,0:T(8,128)}, f32[2,128,512]{2,1,0:T(8,128)S(1)}, u32[]{:S(2)}, u32[]{:S(2)}) collective-permute-start(f32[2,128,512]{2,1,0:T(8,128)} %get-tuple-element.39), channel_id=1, source_target_pairs={{0,6},{1,97},{2,0},{3,99},{4,2},{5,101},{6,4},{7,103},{8,14},{9,10... | collective-permute-start | bytes 1572872 | tf_op jit(solution)/shard_map/ppermute | solution.py:48
  13.5 11.5 %collective-permute-start.3 = (f32[2,128,512]{2,1,0:T(8,128)}, f32[2,128,512]{2,1,0:T(8,128)S(1)}, u32[]{:S(2)}, u32[]{:S(2)}) collective-permute-start(f32[2,128,512]{2,1,0:T(8,128)} %get-tuple-element.49), channel_id=1, source_target_pairs={{0,6},{1,97},{2,0},{3,99},{4,2},{5,101},{6,4},{7,103},{8,14},{9,10... | collective-permute-start | bytes 1572872 | tf_op jit(solution)/shard_map/ppermute | solution.py:48
  15.0 10.0 %collective-permute-start.4 = (f32[2,128,512]{2,1,0:T(8,128)}, f32[2,128,512]{2,1,0:T(8,128)S(1)}, u32[]{:S(2)}, u32[]{:S(2)}) collective-permute-start(f32[2,128,512]{2,1,0:T(8,128)} %get-tuple-element.51), channel_id=1, source_target_pairs={{0,2},{1,33},{2,4},{3,35},{4,6},{5,37},{6,0},{7,39},{8,10},{9,41},... | collective-permute-start | bytes 1572872 | tf_op jit(solution)/shard_map/ppermute | solution.py:48
  16.8 44.9 %slice-start = ((s8[8388608]{0:T(1024)(128)(4,1)}), s8[4194304]{0:T(1024)(128)(4,1)S(1)}, s32[]{:S(2)}) async-start(s8[8388608]{0:T(1024)(128)(4,1)} %bitcast.31), calls=%async_computation | async-start | bytes 8388608
  16.8 13.6 %collective-permute-start.2 = (f32[2,128,512]{2,1,0:T(8,128)S(1)}, f32[2,128,512]{2,1,0:T(8,128)S(1)}, u32[]{:S(2)}, u32[]{:S(2)}) collective-permute-start(f32[2,128,512]{2,1,0:T(8,128)S(1)} %get-tuple-element.40), channel_id=1, source_target_pairs={{0,2},{1,33},{2,4},{3,35},{4,6},{5,37},{6,0},{7,39},{8,10},{9,41},... | collective-permute-start | bytes 1572872 | tf_op jit(solution)/shard_map/ppermute | solution.py:48
  20.1 10.3 %collective-permute-start.5 = (f32[2,128,512]{2,1,0:T(8,128)S(1)}, f32[2,128,512]{2,1,0:T(8,128)S(1)}, u32[]{:S(2)}, u32[]{:S(2)}) collective-permute-start(f32[2,128,512]{2,1,0:T(8,128)S(1)} %get-tuple-element.52), channel_id=1, source_target_pairs={{0,6},{1,97},{2,0},{3,99},{4,2},{5,101},{6,4},{7,103},{8,14},{9,10... | collective-permute-start | bytes 1572872 | tf_op jit(solution)/shard_map/ppermute | solution.py:48
  22.0 39.7 %slice-start.1 = ((s8[8388608]{0:T(1024)(128)(4,1)}), s8[4194304]{0:T(1024)(128)(4,1)S(1)}, s32[]{:S(2)}) async-start(s8[8388608]{0:T(1024)(128)(4,1)} %bitcast.31), calls=%async_computation.1 | async-start | bytes 8388608
  30.6 6.8 %collective-permute-start.6 = (f32[128,512]{1,0:T(8,128)S(1)}, f32[128,512]{1,0:T(8,128)S(1)}, u32[]{:S(2)}, u32[]{:S(2)}) collective-permute-start(f32[128,512]{1,0:T(8,128)S(1)} %get-tuple-element.54), channel_id=1, source_target_pairs={{0,8},{1,3},{2,10},{3,5},{4,12},{5,7},{6,14},{7,1},{8,16},{9,11},{... | collective-permute-start | bytes 786440 | tf_op jit(solution)/shard_map/ppermute | solution.py:48
  31.6 9.6 %collective-permute-start.7 = (f32[128,512]{1,0:T(8,128)S(1)}, f32[128,512]{1,0:T(8,128)S(1)}, u32[]{:S(2)}, u32[]{:S(2)}) collective-permute-start(f32[128,512]{1,0:T(8,128)S(1)} %get-tuple-element.55), channel_id=1, source_target_pairs={{0,16},{1,5},{2,18},{3,7},{4,20},{5,1},{6,22},{7,3},{8,24},{9,13},... | collective-permute-start | bytes 786440 | tf_op jit(solution)/shard_map/ppermute | solution.py:48
  34.3 6.9 %collective-permute-start.8 = (f32[128,512]{1,0:T(8,128)S(1)}, f32[128,512]{1,0:T(8,128)S(1)}, u32[]{:S(2)}, u32[]{:S(2)}) collective-permute-start(f32[128,512]{1,0:T(8,128)S(1)} %get-tuple-element.56), channel_id=1, source_target_pairs={{0,24},{1,7},{2,26},{3,1},{4,28},{5,3},{6,30},{7,5},{8,0},{9,15},{... | collective-permute-start | bytes 786440 | tf_op jit(solution)/shard_map/ppermute | solution.py:48
  41.2 6.8 %collective-permute-start.10 = (f32[128,512]{1,0:T(8,128)S(1)}, f32[128,512]{1,0:T(8,128)S(1)}, u32[]{:S(2)}, u32[]{:S(2)}) collective-permute-start(f32[128,512]{1,0:T(8,128)S(1)} %plain_sum.2.own_ref), channel_id=1, source_target_pairs={{0,64},{1,17},{2,66},{3,19},{4,68},{5,21},{6,70},{7,23},{8,72},{9,... | collective-permute-start | bytes 786440 | tf_op jit(solution)/shard_map/ppermute | solution.py:48
  43.9 7.3 %collective-permute-start.11 = (f32[128,512]{1,0:T(8,128)S(1)}, f32[128,512]{1,0:T(8,128)S(1)}, u32[]{:S(2)}, u32[]{:S(2)}) collective-permute-start(f32[128,512]{1,0:T(8,128)S(1)} %plain_sum.2.own_ref), channel_id=1, source_target_pairs={{0,96},{1,25},{2,98},{3,27},{4,100},{5,29},{6,102},{7,31},{8,104},... | collective-permute-start | bytes 786440 | tf_op jit(solution)/shard_map/ppermute | solution.py:48
  44.7 6.7 %collective-permute-start.9 = (f32[128,512]{1,0:T(8,128)S(1)}, f32[128,512]{1,0:T(8,128)S(1)}, u32[]{:S(2)}, u32[]{:S(2)}) collective-permute-start(f32[128,512]{1,0:T(8,128)S(1)} %plain_sum.2.own_ref), channel_id=1, source_target_pairs={{0,32},{1,9},{2,34},{3,11},{4,36},{5,13},{6,38},{7,15},{8,40},{9,1... | collective-permute-start | bytes 786440 | tf_op jit(solution)/shard_map/ppermute | solution.py:48
  52.0 5.4 %collective-permute-start.12 = (f32[64,640]{1,0:T(8,128)S(1)}, f32[64,640]{1,0:T(8,128)S(1)}, u32[]{:S(2)}, u32[]{:S(2)}) collective-permute-start(f32[64,640]{1,0:T(8,128)S(1)} %amplitudes.1.own_ref), channel_id=1, source_target_pairs={{0,8},{1,3},{2,10},{3,5},{4,12},{5,7},{6,14},{7,1},{8,16},{9,11},{... | collective-permute-start | bytes 491528 | tf_op jit(solution)/shard_map/ppermute | solution.py:48
  53.4 6.1 %collective-permute-start.13 = (f32[64,640]{1,0:T(8,128)S(1)}, f32[64,640]{1,0:T(8,128)S(1)}, u32[]{:S(2)}, u32[]{:S(2)}) collective-permute-start(f32[64,640]{1,0:T(8,128)S(1)} %amplitudes.1.own_ref), channel_id=1, source_target_pairs={{0,16},{1,5},{2,18},{3,7},{4,20},{5,1},{6,22},{7,3},{8,24},{9,13},... | collective-permute-start | bytes 491528 | tf_op jit(solution)/shard_map/ppermute | solution.py:48
  55.1 4.7 %collective-permute-start.14 = (f32[64,640]{1,0:T(8,128)S(1)}, f32[64,640]{1,0:T(8,128)S(1)}, u32[]{:S(2)}, u32[]{:S(2)}) collective-permute-start(f32[64,640]{1,0:T(8,128)S(1)} %amplitudes.1.own_ref), channel_id=1, source_target_pairs={{0,24},{1,7},{2,26},{3,1},{4,28},{5,3},{6,30},{7,5},{8,0},{9,15},{... | collective-permute-start | bytes 491528 | tf_op jit(solution)/shard_map/ppermute | solution.py:48
  59.8 8.5 %collective-permute-start.17 = (f32[64,2176]{1,0:T(8,128)S(1)}, f32[64,2176]{1,0:T(8,128)S(1)}, u32[]{:S(2)}, u32[]{:S(2)}) collective-permute-start(f32[64,2176]{1,0:T(8,128)S(1)} %join.1.amp_ref), channel_id=1, source_target_pairs={{0,6},{1,97},{2,0},{3,99},{4,2},{5,101},{6,4},{7,103},{8,14},{9,10... | collective-permute-start | bytes 1671176 | tf_op jit(solution)/shard_map/ppermute | solution.py:48
  61.0 10.0 %collective-permute-start.16 = (f32[64,2176]{1,0:T(8,128)S(1)}, f32[64,2176]{1,0:T(8,128)S(1)}, u32[]{:S(2)}, u32[]{:S(2)}) collective-permute-start(f32[64,2176]{1,0:T(8,128)S(1)} %join.1.amp_ref), channel_id=1, source_target_pairs={{0,4},{1,65},{2,6},{3,67},{4,0},{5,69},{6,2},{7,71},{8,12},{9,73},... | collective-permute-start | bytes 1671176 | tf_op jit(solution)/shard_map/ppermute | solution.py:48
  61.1 15.9 %collective-permute-start.15 = (f32[64,2176]{1,0:T(8,128)S(1)}, f32[64,2176]{1,0:T(8,128)S(1)}, u32[]{:S(2)}, u32[]{:S(2)}) collective-permute-start(f32[64,2176]{1,0:T(8,128)S(1)} %join.1.amp_ref), channel_id=1, source_target_pairs={{0,2},{1,33},{2,4},{3,35},{4,6},{5,37},{6,0},{7,39},{8,10},{9,41},... | collective-permute-start | bytes 1671176 | tf_op jit(solution)/shard_map/ppermute | solution.py:48
  77.0 9.7 %collective-permute-start.18 = (f32[64,128]{1,0:T(8,128)S(1)}, f32[64,128]{1,0:T(8,128)S(1)}, u32[]{:S(2)}, u32[]{:S(2)}) collective-permute-start(f32[64,128]{1,0:T(8,128)S(1)} %plain_sum.3.here_ref), channel_id=1, source_target_pairs={{0,1},{1,0},{2,3},{3,2},{4,5},{5,4},{6,7},{7,6},{8,9},{9,8},{10,11... | collective-permute-start | bytes 98312 | tf_op jit(solution)/shard_map/ppermute | solution.py:52
